TPU v7x, 32 devices: a whole 2x2x4 slice. The times are simulated.
32 devices in a mesh: ctx: 8 (over y, x, core), tp: 4 (over z).
Axes of the slice: x: 2, y: 2, z: 4, core: 2. Of those that a mesh axis runs over, the one named last changes fastest.
Arguments:
- hidden: bfloat16 [2048, 5120], P('ctx', 'tp'), may hold values from -6 to 6
- queries: bfloat16 [2048, 5120], P('ctx', 'tp'), may hold values from -28 to 28
- key_weight: bfloat16 [5120, 1024], P(None, 'tp'), may hold values from -0.078125 to 0.078125
- value_weight: bfloat16 [5120, 1024], P(None, 'tp'), may hold values from -0.078125 to 0.078125
- parents: int32 [16], replicated, may hold values from -1 to 14, as said below
- upstream: bfloat16 [2048, 5120], P('ctx', 'tp'), may hold values from -6 to 6
Outputs:
- attention: bfloat16 [2048, 5120], P('ctx', 'tp')
- query_grad: bfloat16 [2048, 5120], P('ctx', 'tp')
- hidden_grad: bfloat16 [2048, 5120], P('ctx', 'tp')
- key_weight_grad: float32 [5120, 1024], P('ctx', 'tp')
- value_weight_grad: float32 [5120, 1024], P('ctx', 'tp')
Inputs may be any that keep to these rules, and one draw needn't show every extreme that they name: Node blocks lie in depth-first order: parents[b] < b is the parent of block b for b > 0, parents[0] = -1 and block 0 is the only root; no root-to-leaf path holds more than 8 blocks; the last 7 blocks form one chain below block 0, so that the last block's path holds exactly 8 blocks.
All inputs are finite; a program needn't handle non-finite values.
Results may differ from a plain program's by a relative error of at most 0.023.
The roundings to bfloat16 on the way count: a program that leaves them out, or rounds other values in their place, can miss the bound.
Values may be sent and summed in bfloat16 or wider, within the bound.
A program may use at most 128 MiB of HBM per device.

v0:
```python
from functools import partial
import math

import jax
import jax.numpy as jnp
from jax import lax
from jax.sharding import PartitionSpec as P

HD = 128
BLOCK = 128
DEPTH = 8


THETA = 1000000.0
NEGATIVE = -1e30
HIGHEST = lax.Precision.HIGHEST


def tree_tables(parents, block_total, depth_slots):
    indices = jnp.arange(block_total, dtype=jnp.int32)
    parent_link = (parents[:, None] == indices[None, :]).astype(jnp.float32)
    closure = jnp.eye(block_total, dtype=jnp.float32) + parent_link
    for repeat in range(depth_slots.bit_length()):
        closure = jnp.minimum(
            jnp.dot(closure, closure, precision=HIGHEST, preferred_element_type=jnp.float32), 1.0
        )
    closure_int = closure.astype(jnp.int32)
    depths = jnp.sum(closure_int, axis=1) - 1
    levels = jnp.arange(depth_slots, dtype=jnp.int32)
    select = closure_int[:, :, None] * (depths[None, :, None] == levels[None, None, :]).astype(
        jnp.int32
    )
    path_ids = jnp.sum(select * indices[None, :, None], axis=1) + jnp.sum(select, axis=1) - 1
    return (depths, path_ids)


def rope_angles(depths, block_len, head_width):
    offset = jnp.arange(block_len, dtype=jnp.int32)
    position = (depths[:, None] * block_len + offset[None, :]).astype(jnp.float32)
    midpoint = head_width // 2
    frequency = jnp.exp(
        jnp.arange(midpoint, dtype=jnp.float32) * (-2.0 * math.log(THETA) / head_width)
    )
    angles = position[:, :, None] * frequency[None, None, :]
    return (jnp.cos(angles), jnp.sin(angles))


def rotate_pairs(fields, cosine, sine_table, direction):
    midpoint = fields.shape[-1] // 2
    leading = fields[..., :midpoint]
    trailing = fields[..., midpoint:]
    cos_part = cosine[:, :, None, :]
    sin_part = direction * sine_table[:, :, None, :]
    return jnp.concatenate(
        [leading * cos_part - trailing * sin_part, trailing * cos_part + leading * sin_part],
        axis=-1,
    )


def allowed_mask(depths, block_len, slot_count):
    query_pos = jnp.arange(block_len, dtype=jnp.int32)
    key_index = jnp.arange(slot_count * block_len, dtype=jnp.int32)
    key_slot = key_index // block_len
    key_offset = key_index % block_len
    earlier = key_slot[None, None, :] < depths[:, None, None]
    itself = (key_slot[None, None, :] == depths[:, None, None]) & (
        key_offset[None, None, :] <= query_pos[None, :, None]
    )
    return earlier | itself


def attend_block(query_blocks, key_rows, value_rows, allowed, upstream_blocks, score_scale):
    scores = (
        jnp.einsum("bqhgd,bkhd->bhgqk", query_blocks, key_rows, preferred_element_type=jnp.float32)
        * score_scale
    )
    scores = jnp.where(allowed[:, None, None], scores, NEGATIVE)
    maximum = jnp.max(scores, axis=-1, keepdims=True)
    weights = jnp.exp(scores - maximum)
    totals = jnp.sum(weights, axis=-1, keepdims=True)
    mixed_rows = jnp.einsum(
        "bhgqk,bkhd->bqhgd",
        weights.astype(jnp.bfloat16),
        value_rows,
        preferred_element_type=jnp.float32,
    )
    totals_rows = jnp.transpose(totals, (0, 3, 1, 2, 4))
    output = (mixed_rows / totals_rows).astype(jnp.bfloat16)
    logsum = maximum + jnp.log(totals)
    deltas = jnp.sum(upstream_blocks.astype(jnp.float32) * output.astype(jnp.float32), axis=-1)
    deltas = jnp.transpose(deltas, (0, 2, 3, 1))[..., None]
    probabilities = jnp.exp(scores - logsum)
    value_grad = jnp.einsum(
        "bhgqk,bqhgd->bkhd",
        probabilities.astype(jnp.bfloat16),
        upstream_blocks,
        preferred_element_type=jnp.float32,
    )
    prob_grad = jnp.einsum(
        "bqhgd,bkhd->bhgqk", upstream_blocks, value_rows, preferred_element_type=jnp.float32
    )
    score_grad = (probabilities * (prob_grad - deltas)).astype(jnp.bfloat16)
    query_grad = (
        jnp.einsum("bhgqk,bkhd->bqhgd", score_grad, key_rows, preferred_element_type=jnp.float32)
        * score_scale
    ).astype(jnp.bfloat16)
    key_grad = (
        jnp.einsum(
            "bhgqk,bqhgd->bkhd", score_grad, query_blocks, preferred_element_type=jnp.float32
        )
        * score_scale
    )
    return (output, query_grad, key_grad, value_grad)


def shards(hidden, queries, key_weight, value_weight, parents, upstream):
    local_rows = hidden.shape[0]
    blocks = local_rows // BLOCK
    block_total = parents.shape[0]
    key_width = key_weight.shape[1]
    key_heads = key_width // HD
    groups = queries.shape[1] // key_width
    pair_width = 2 * key_width
    score_scale = 1.0 / math.sqrt(HD)
    first_block = lax.axis_index("ctx") * blocks
    depth_all, path_all = tree_tables(parents, block_total, DEPTH)
    depths = lax.dynamic_slice_in_dim(depth_all, first_block, blocks, 0)
    path_ids = lax.dynamic_slice_in_dim(path_all, first_block, blocks, 0)
    cosine, sine_table = rope_angles(depths, BLOCK, HD)
    features = lax.all_gather(hidden, "tp", axis=1, tiled=True)
    key_linear = jnp.dot(features, key_weight, preferred_element_type=jnp.float32).reshape(
        blocks, BLOCK, key_heads, HD
    )
    key_rotated = (
        rotate_pairs(key_linear, cosine, sine_table, 1.0)
        .astype(jnp.bfloat16)
        .reshape(local_rows, key_width)
    )
    value_rows = jnp.dot(features, value_weight, preferred_element_type=jnp.float32).astype(
        jnp.bfloat16
    )
    key_value = jnp.concatenate([key_rotated, value_rows], axis=1)
    gathered = lax.all_gather(key_value, "ctx", axis=0, tiled=True).reshape(
        block_total, BLOCK, pair_width
    )
    slot_rows = gathered[jnp.clip(path_ids, 0, block_total - 1)]
    query_blocks = queries.reshape(blocks, BLOCK, key_heads, groups, HD)
    upstream_blocks = upstream.reshape(blocks, BLOCK, key_heads, groups, HD)

    def attend_slots(slot_count):
        chosen = slot_rows[:, :slot_count].reshape(blocks, slot_count * BLOCK, pair_width)
        key_part = chosen[..., :key_width].reshape(blocks, slot_count * BLOCK, key_heads, HD)
        value_part = chosen[..., key_width:].reshape(blocks, slot_count * BLOCK, key_heads, HD)
        allowed = allowed_mask(depths, BLOCK, slot_count)
        output, query_grad, key_grad, value_grad = attend_block(
            query_blocks, key_part, value_part, allowed, upstream_blocks, score_scale
        )
        slot_grads = jnp.concatenate(
            [
                key_grad.reshape(blocks, slot_count, BLOCK, key_width),
                value_grad.reshape(blocks, slot_count, BLOCK, key_width),
            ],
            axis=-1,
        )
        slot_grads = jnp.pad(slot_grads, ((0, 0), (0, DEPTH - slot_count), (0, 0), (0, 0)))
        return (
            output.reshape(local_rows, groups * key_width),
            query_grad.reshape(local_rows, groups * key_width),
            slot_grads,
        )

    needed = jnp.max(depths) + 1
    bucket = (needed > DEPTH // 4).astype(jnp.int32) + (needed > DEPTH // 2).astype(jnp.int32)
    bucket_sizes = [DEPTH // 4, DEPTH // 2, DEPTH]
    attention, query_grad, slot_grads = lax.switch(
        bucket, [partial(attend_slots, slot_count) for slot_count in bucket_sizes]
    )
    flat_grads = slot_grads.reshape(blocks * DEPTH, BLOCK * pair_width)
    block_targets = path_ids.reshape(blocks * DEPTH)
    block_count = local_rows * lax.axis_size("ctx") // BLOCK
    selector = (block_targets[None, :] == jnp.arange(block_count, dtype=jnp.int32)[:, None]).astype(
        jnp.float32
    )
    pair_grads = lax.psum_scatter(
        jnp.dot(
            selector, flat_grads, precision=HIGHEST, preferred_element_type=jnp.float32
        ).reshape(local_rows * lax.axis_size("ctx"), pair_width),
        "ctx",
        scatter_dimension=0,
        tiled=True,
    )
    key_total = pair_grads[:, :key_width].reshape(blocks, BLOCK, key_heads, HD)
    key_linear_grad = (
        rotate_pairs(key_total, cosine, sine_table, -1.0)
        .astype(jnp.bfloat16)
        .reshape(local_rows, key_width)
    )
    value_grad_rows = pair_grads[:, key_width:].astype(jnp.bfloat16)
    grad_pairs = jnp.concatenate([key_linear_grad, value_grad_rows], axis=1)
    hidden_columns = lax.all_to_all(features, "ctx", split_axis=1, concat_axis=0, tiled=True)
    weight_grads = jnp.einsum(
        "tc,tw->cw",
        hidden_columns,
        lax.all_gather(grad_pairs, "ctx", axis=0, tiled=True),
        preferred_element_type=jnp.float32,
    )
    partial_input = jnp.einsum(
        "tw,dw->td", key_linear_grad, key_weight, preferred_element_type=jnp.float32
    )
    partial_input = partial_input + jnp.einsum(
        "tw,dw->td", value_grad_rows, value_weight, preferred_element_type=jnp.float32
    )
    hidden_grad = lax.psum_scatter(
        partial_input.astype(jnp.bfloat16), "tp", scatter_dimension=1, tiled=True
    )
    return (
        attention,
        query_grad,
        hidden_grad,
        weight_grads[:, :key_width],
        weight_grads[:, key_width:],
    )


def solution(mesh):
    return jax.shard_map(
        shards,
        mesh=mesh,
        in_specs=(
            P("ctx", "tp"),
            P("ctx", "tp"),
            P(None, "tp"),
            P(None, "tp"),
            P(),
            P("ctx", "tp"),
        ),
        out_specs=(P("ctx", "tp"), P("ctx", "tp"), P("ctx", "tp"), P("ctx", "tp"), P("ctx", "tp")),
        check_vma=False,
    )
```

profile of v0, /device:TPU:0, one launch (start us, length us, event | category | flops | bytes accessed | tf_op | source)
XLA Modules:
  0.0 386.3 jit_solution(12864037735893717116)
XLA Ops:
  7.2 2.3 copy.216
  12.5 55.2 %all-gather.4.cloned.1.call-done = bf16[256,5120]{0,1:T(8,128)(2,1)} async-done(((bf16[256,1280]{0,1:T(8,128)(2,1)}), bf16[256,5120]{0,1:T(8,128)(2,1)}) %all-gather.4.cloned.1.call-update) | async-done | bytes 2621456 | tf_op jit(solution)/shard_map/all_gather | solution.py:130
  67.7 2.6 fusion.125
  71.5 3.7 convolution_convert_fusion
  78.5 24.6 %all-gather.6.cloned.1.call-done = bf16[2048,512]{0,1:T(8,128)(2,1)} async-done(((bf16[256,512]{0,1:T(8,128)(2,1)}), bf16[2048,512]{0,1:T(8,128)(2,1)}) %all-gather.6.cloned.1.call-update) | async-done | bytes 2097168 | tf_op jit(solution)/shard_map/all_gather | solution.py:143
  103.1 69.6 %conditional.1 = (f32[16,65536]{1,0:T(8,128)}, bf16[256,1280]{1,0:T(8,128)(2,1)S(1)}, bf16[256,1280]{1,0:T(8,128)(2,1)}) conditional(s32[]{:T(128)} %clamp.4, (s32[2]{0:T(128)S(1)}, bf16[2048,512]{0,1:T(8,128)(2,1)}, s32[]{:T(128)}, bf16[256,1280]{1,0:T(8,128)(2,1)S(1)}, bf16[256,1280]{1,0:T(8,128)(2,1)}, ...), branch_computations={%region_4.8_spmd.clone, %region_8.12_spmd.clone, %region_12.16_spm... | conditional | flops 4086446080 | bytes 228734272 | solution.py:175
  103.1 3.9 %copy.305 = bf16[2048,512]{1,0:T(8,128)(2,1)} copy(bf16[2048,512]{0,1:T(8,128)(2,1)} %get-tuple-element.212) | data formatting | bytes 4194304 | tf_op jit(solution)/shard_map
  107.1 3.6 gather_fusion
  116.4 2.0 fusion.119
  124.4 2.0 copy.302
  126.4 3.4 multiply_reduce_fusion
  134.3 2.3 reshape.590
  136.5 2.3 fusion.15
  143.0 4.4 %copy.342 = f32[2,8,128,512]{3,1,2,0:T(8,128)} copy(f32[2,8,128,512]{3,2,1,0:T(8,128)S(1)} %fusion) | data formatting | bytes 8388608 | tf_op jit(solution)/shard_map/cond
  149.6 2.6 reshape.596
  172.7 6.5 %fusion.112 = f32[16,65536]{1,0:T(8,128)} fusion(f32[16,65536]{1,0:T(8,128)} %get-tuple-element.101, s32[16]{0:T(128)} %eq.104), kind=kOutput, calls=%fused_computation.184 | convolution fusion | flops 201326848 | bytes 8388672 | tf_op jit(solution)/shard_map/dot_general | solution.py:185
  179.3 3.9 %reshape.526 = f32[2048,512]{1,0:T(8,128)} reshape(f32[16,65536]{1,0:T(8,128)} %fusion.112) | data formatting | bytes 8388608 | tf_op jit(solution)/shard_map/reshape | solution.py:187
  183.3 93.9 %reduce-scatter.3.cloned.1.call-done = f32[256,512]{1,0:T(8,128)} async-done(((f32[2048,512]{1,0:T(8,128)}), f32[256,512]{1,0:T(8,128)}) %reduce-scatter.3.cloned.1.call-update) | async-done | bytes 524304 | tf_op jit(solution)/shard_map/reduce_scatter | solution.py:184
  282.9 2.4 fusion.106
  285.3 43.4 %all_to_all.19 = bf16[256,8,640]{0,2,1:T(8,128)(2,1)} all-to-all(bf16[256,8,640]{0,2,1:T(8,128)(2,1)} %bitcast.335), channel_id=1, replica_groups=mesh['ctx'=8,'tp'=4] {'ctx'}, dimensions={1} | all-to-all | bytes 5242880 | tf_op jit(solution)/shard_map/all_to_all | solution.py:200
  328.7 4.4 %copy.227 = bf16[8,256,640]{2,1,0:T(8,128)(2,1)} copy(bf16[8,256,640]{1,2,0:T(8,128)(2,1)} %bitcast.319) | data formatting | bytes 5242880 | tf_op jit(solution)/shard_map/all_to_all | solution.py:200
  333.1 4.4 %convolution_bitcast_fusion.3 = f32[640,512]{0,1:T(8,128)S(1)} fusion(bf16[2048,512]{1,0:T(8,128)(2,1)} %all-gather.8.cloned.1.call-done, bf16[2048,640]{1,0:T(8,128)(2,1)} %bitcast.336), kind=kOutput, calls=%fused_computation.154 | convolution fusion | flops 1342177280 | bytes 6029312 | tf_op jit(solution)/shard_map/tc,tw->cw/dot_general | solution.py:201
  338.4 2.2 copy.230
  341.7 37.9 %reduce-scatter.5.cloned.1.call-done = bf16[256,1280]{1,0:T(8,128)(2,1)} async-done(((bf16[256,5120]{1,0:T(8,128)(2,1)}), bf16[256,1280]{1,0:T(8,128)(2,1)}) %reduce-scatter.5.cloned.1.call-update) | async-done | bytes 655376 | tf_op jit(solution)/shard_map/reduce_scatter | solution.py:213
  (103 shorter events, 40.4 us)
Async XLA Ops:
  7.2 60.5 %copy-start = (bf16[5120,256]{1,0:T(8,128)(2,1)S(1)}, bf16[5120,256]{1,0:T(8,128)(2,1)}, u32[]{:S(2)}) copy-start(bf16[5120,256]{1,0:T(8,128)(2,1)} %param.11) | copy-start | bytes 7864324
  7.2 60.5 %all-gather.4.cloned.1.call-start = ((), (), s32[]{:S(2)}) async-start(), calls=%async_computation.3 | async-start | bytes 3276800 | tf_op jit(solution)/shard_map/all_gather | solution.py:130
  9.6 93.5 %all-gather.6.cloned.1.call-start = ((), (), s32[]{:S(2)}) async-start(), calls=%async_computation.4 | async-start | bytes 2359296 | tf_op jit(solution)/shard_map/all_gather | solution.py:143
  12.5 58.0 %copy-start.20 = (f32[2,128,64]{2,1,0:T(8,128)}, f32[2,128,64]{2,1,0:T(8,128)S(1)}, u32[]{:S(2)}) copy-start(f32[2,128,64]{2,1,0:T(8,128)S(1)} %get-tuple-element.283) | copy-start | bytes 196612
  71.5 31.6 %copy-start.9 = (bf16[256,1280]{1,0:T(8,128)(2,1)S(1)}, bf16[256,1280]{1,0:T(8,128)(2,1)}, u32[]{:S(2)}) copy-start(bf16[256,1280]{1,0:T(8,128)(2,1)} %param.10) | copy-start | bytes 1966084
  75.9 201.3 %reduce-scatter.3.cloned.1.call-start = ((), (), s32[]{:S(2)}) async-start(), calls=%async_computation.5 | async-start | bytes 4718592 | tf_op jit(solution)/shard_map/reduce_scatter | solution.py:184
  116.4 6.2 %copy-start.10 = (bf16[256,1280]{1,0:T(8,128)(2,1)S(1)}, bf16[256,1280]{1,0:T(8,128)(2,1)}, u32[]{:S(2)}) copy-start(bf16[256,1280]{1,0:T(8,128)(2,1)} %get-tuple-element.214) | copy-start | bytes 1966084 | tf_op jit(solution)/shard_map/cond
  118.4 1.5 copy-start.2
  118.4 8.0 %copy-start.32 = (f32[2,2,5,128]{3,2,1,0:T(8,128)}, f32[2,2,5,128]{3,2,1,0:T(8,128)S(1)}, u32[]{:S(2)}) copy-start(f32[2,2,5,128]{3,2,1,0:T(8,128)S(1)} %get-tuple-element.255) | copy-start | bytes 30724 | tf_op jit(solution)/shard_map/cond
  126.4 3.5 copy-start.34
  126.4 4.3 %copy-start.3 = (f32[2,2,5,128,256]{3,4,2,1,0:T(8,128)S(1)}, f32[2,2,5,128,256]{3,4,2,1,0:T(8,128)}, u32[]{:S(2)}) copy-start(f32[2,2,5,128,256]{3,4,2,1,0:T(8,128)} %copy-done.2) | copy-start | bytes 7864324 | tf_op jit(solution)/shard_map/cond
  126.4 4.3 %copy-start.22 = (bf16[2,256,256]{1,2,0:T(8,128)(2,1)S(1)}, bf16[2,256,256]{1,2,0:T(8,128)(2,1)}, u32[]{:S(2)}) copy-start(bf16[2,256,256]{1,2,0:T(8,128)(2,1)} %copy.333) | copy-start | bytes 786436 | tf_op jit(solution)/shard_map/cond
  129.8 2.7 copy-start.14
  131.4 1.1 copy-start.6
  143.0 4.4 %copy-start.7 = (bf16[2,2,5,128,256]{3,4,2,1,0:T(8,128)(2,1)S(1)}, bf16[2,2,5,128,256]{3,4,2,1,0:T(8,128)(2,1)}, u32[]{:S(2)}) copy-start(bf16[2,2,5,128,256]{3,4,2,1,0:T(8,128)(2,1)} %copy-done.6) | copy-start | bytes 3932164 | tf_op jit(solution)/shard_map/cond
  147.4 4.7 %copy-start.25 = (bf16[2,128,2,5,128]{1,4,3,2,0:T(8,128)(2,1)S(1)}, bf16[2,128,2,5,128]{1,4,3,2,0:T(8,128)(2,1)}, u32[]{:S(2)}) copy-start(bf16[2,128,2,5,128]{1,4,3,2,0:T(8,128)(2,1)} %get-tuple-element.258) | copy-start | bytes 1966084 | tf_op jit(solution)/shard_map/cond
  172.7 6.5 %copy-start.29 = (bf16[256,1280]{1,0:T(8,128)(2,1)}, bf16[256,1280]{1,0:T(8,128)(2,1)S(1)}, u32[]{:S(2)}) copy-start(bf16[256,1280]{1,0:T(8,128)(2,1)S(1)} %get-tuple-element.194) | copy-start | bytes 1966084
  183.2 95.1 %copy-start.21 = (f32[2,128,64]{2,1,0:T(8,128)S(1)}, f32[2,128,64]{2,1,0:T(8,128)}, u32[]{:S(2)}) copy-start(f32[2,128,64]{2,1,0:T(8,128)} %copy-done.20) | copy-start | bytes 196612
  183.2 95.1 %copy-start.31 = (f32[2,128,64]{2,1,0:T(8,128)S(1)}, f32[2,128,64]{2,1,0:T(8,128)}, u32[]{:S(2)}) copy-start(f32[2,128,64]{2,1,0:T(8,128)} %get-tuple-element.281) | copy-start | bytes 196612
  183.2 149.9 %all-gather.8.cloned.1.call-start = ((), (), s32[]{:S(2)}) async-start(), calls=%async_computation.7 | async-start | bytes 2359296 | tf_op jit(solution)/shard_map/all_gather | solution.py:204
  280.9 1.0 copy-start.24
  280.9 98.6 %reduce-scatter.5.cloned.1.call-start = ((), (), s32[]{:S(2)}) async-start(), calls=%async_computation.6 | async-start | bytes 3276800 | tf_op jit(solution)/shard_map/reduce_scatter | solution.py:213
  281.0 1.9 copy-start.19
Sparse Core Ops, SparseCore 0:
  10.2 57.4 all-gather.3
  76.1 26.9 all-gather.5
  183.3 93.8 reduce-scatter.2
  281.1 43.4 all-gather.7
  327.4 52.1 reduce-scatter.4
where the time goes:
time: 393 us; the launch traced here: 386 us
  waiting for transfers between devices  212 us (54%)
  local copies, waits for them, and re-layouts  57.2 us (15%)
  blocking collectives  43.4 us (11%)
  matrix products  31.5 us (8%)
  loops' own time  17.2 us (4%)
  between operations  14.9 us (4%)
  other arithmetic  10.2 us (3%)
    reduce_scatter x1, waiting for transfers between devices, shards(): lax.psum_scatter(jnp.dot(selector, flat_grads, precision=HIGHEST, preferr...  93.9 us
    all_gather x1, waiting for transfers between devices, shards(): features = lax.all_gather(hidden, 'tp', axis=1, tiled=True)  55.2 us
    all_to_all x1, blocking collectives, shards(): lax.all_to_all(features, 'ctx', split_axis=1, concat_axis=0, tiled=True)  43.4 us
    reduce_scatter x1, waiting for transfers between devices, shards(): lax.psum_scatter(partial_input.astype(jnp.bfloat16), 'tp', scatter_dimens...  37.9 us
    all_gather x1, waiting for transfers between devices, shards(): lax.all_gather(key_value, 'ctx', axis=0, tiled=True)  24.6 us
    cond x27, local copies, waits for them, and re-layouts  17.5 us
    another operation x1, loops' own time, shards(): lax.switch(bucket, [partial(attend_slots, slot_count) for slot_count in b...  17.2 us
  transfers between devices with their start and end apart: 5, of which 4 were waited for; matrix products, arithmetic and copies ran while one was open for 5% of the time, Pallas kernels for 0%

commit v1 on v0

v1 whole, which is shorter than its diff:
```python
import math

import jax
import jax.numpy as jnp
from jax import lax
from jax.experimental import pallas as pl
from jax.experimental.pallas import tpu as pltpu
from jax.sharding import PartitionSpec as P

HD = 128
BLOCK = 128
DEPTH = 8
THETA = 1000000.0
NEGATIVE = -1e30
VMEM_LIMIT = 56 * 1024 * 1024
MESH = pl.DeviceIdType.MESH


def walk(parents_ref, block):
    chain = [block]
    for _ in range(DEPTH - 1):
        last = chain[-1]
        above = parents_ref[jnp.maximum(last, 0)]
        chain.append(jnp.where(last > 0, above, -1))
    depth = jnp.int32(0)
    for node in chain[1:]:
        depth = depth + jnp.where(node >= 0, 1, 0)
    path = []
    for level in range(DEPTH):
        found = jnp.int32(0)
        for hop in range(DEPTH):
            found = found + jnp.where(depth - hop == level, chain[hop], 0)
        path.append(found)
    return depth, path


def dot_f32(left, right, left_dim, right_dim):
    return lax.dot_general(
        left, right, (((left_dim,), (right_dim,)), ((), ())), preferred_element_type=jnp.float32
    )


def attend(parents_ref, kv_ref, q_ref, u_ref, att_ref, qg_ref, part_ref, s_ref, grads_ref):
    rows, width = q_ref.shape
    blocks = rows // BLOCK
    pair_width = kv_ref.shape[1]
    key_width = pair_width // 2
    key_heads = key_width // HD
    groups = width // key_width
    lanes = groups * BLOCK
    step = 2 * BLOCK
    steps = DEPTH // 2
    scale = 1.0 / math.sqrt(HD)
    first = lax.axis_index("ctx") * blocks

    def one_block(b, carry):
        depth, path = walk(parents_ref, first + b)
        row0 = pl.multiple_of(b * BLOCK, BLOCK)
        here = pl.ds(row0, BLOCK)
        key_row = lax.broadcasted_iota(jnp.int32, (step, lanes), 0)
        query_row = lax.broadcasted_iota(jnp.int32, (step, lanes), 1) % BLOCK
        limit = depth * BLOCK + query_row - key_row
        for g in range(key_heads):
            def head_cols(h):
                return slice((g * groups + h) * HD, (g * groups + h + 1) * HD)

            key_cols = slice(g * HD, (g + 1) * HD)
            value_cols = slice(key_width + g * HD, key_width + (g + 1) * HD)
            q = jnp.concatenate([q_ref[here, head_cols(h)] for h in range(groups)], axis=0)
            u = jnp.concatenate([u_ref[here, head_cols(h)] for h in range(groups)], axis=0)
            u_t = u.astype(jnp.float32).T

            def pair(p, cols):
                return jnp.concatenate(
                    [
                        kv_ref[pl.ds(pl.multiple_of(path[2 * p + i] * BLOCK, BLOCK), BLOCK), cols]
                        for i in range(2)
                    ],
                    axis=0,
                )

            top = jnp.full((1, lanes), NEGATIVE, jnp.float32)
            for p in range(steps):
                s = dot_f32(pair(p, key_cols), q, 1, 1) * scale
                s = jnp.where(limit >= p * step, s, NEGATIVE)
                s_ref[p] = s
                top = jnp.maximum(top, jnp.max(s, axis=0, keepdims=True))
            totals = jnp.zeros((1, lanes), jnp.float32)
            mixed = jnp.zeros((HD, lanes), jnp.float32)
            for p in range(steps):
                w = jnp.exp(s_ref[p] - top)
                s_ref[p] = w
                totals = totals + jnp.sum(w, axis=0, keepdims=True)
                mixed = mixed + dot_f32(pair(p, value_cols), w.astype(jnp.bfloat16), 0, 0)
            out_t = (mixed / totals).astype(jnp.bfloat16).astype(jnp.float32)
            out = out_t.T.astype(jnp.bfloat16)
            for h in range(groups):
                att_ref[here, head_cols(h)] = out[h * BLOCK : (h + 1) * BLOCK]
            deltas = jnp.sum(out_t * u_t, axis=0, keepdims=True)
            inverse = 1.0 / totals
            query_grad = jnp.zeros((HD, lanes), jnp.float32)
            for p in range(steps):
                prob = s_ref[p] * inverse
                value_part = dot_f32(prob.astype(jnp.bfloat16), u, 1, 0)
                prob_grad = dot_f32(pair(p, value_cols), u, 1, 1)
                ds = (prob * (prob_grad - deltas)).astype(jnp.bfloat16)
                key_part = dot_f32(ds, q, 1, 0) * scale
                query_grad = query_grad + dot_f32(pair(p, key_cols), ds, 0, 0)
                for i in range(2):
                    grads_ref[b, 2 * p + i, :, key_cols] = key_part[i * BLOCK : (i + 1) * BLOCK]
                    grads_ref[b, 2 * p + i, :, value_cols] = value_part[i * BLOCK : (i + 1) * BLOCK]
            qg = (query_grad * scale).T.astype(jnp.bfloat16)
            for h in range(groups):
                qg_ref[here, head_cols(h)] = qg[h * BLOCK : (h + 1) * BLOCK]
        return carry

    lax.fori_loop(0, blocks, one_block, 0)

    paths = [walk(parents_ref, first + b) for b in range(blocks)]
    block_total = part_ref.shape[0] // BLOCK

    def one_target(target, carry):
        total = jnp.zeros((BLOCK, pair_width), jnp.float32)
        for b in range(blocks):
            depth, path = paths[b]
            slot = jnp.int32(0)
            hits = jnp.int32(0)
            for level in range(DEPTH):
                hit = jnp.where((path[level] == target) & (depth >= level), 1, 0)
                slot = slot + hit * level
                hits = hits + hit
            total = total + jnp.where(hits > 0, grads_ref[b, slot], 0.0)
        part_ref[pl.ds(pl.multiple_of(target * BLOCK, BLOCK), BLOCK), :] = total.astype(
            part_ref.dtype
        )
        return carry

    lax.fori_loop(0, block_total, one_target, 0)


def attention_call(parents, kv, queries, upstream, part_dtype):
    rows, width = queries.shape
    blocks = rows // BLOCK
    pair_width = kv.shape[1]
    groups = width // (pair_width // 2)
    vmem = pl.BlockSpec(memory_space=pltpu.VMEM)
    return pl.pallas_call(
        attend,
        name="attend",
        out_shape=(
            jax.ShapeDtypeStruct(queries.shape, jnp.bfloat16),
            jax.ShapeDtypeStruct(queries.shape, jnp.bfloat16),
            jax.ShapeDtypeStruct(kv.shape, part_dtype),
        ),
        in_specs=[pl.BlockSpec(memory_space=pltpu.SMEM), vmem, vmem, vmem],
        out_specs=(vmem, vmem, vmem),
        scratch_shapes=[
            pltpu.VMEM((DEPTH // 2, 2 * BLOCK, groups * BLOCK), jnp.float32),
            pltpu.VMEM((blocks, DEPTH, BLOCK, pair_width), jnp.float32),
        ],
        compiler_params=pltpu.CompilerParams(vmem_limit_bytes=VMEM_LIMIT),
    )(parents, kv, queries, upstream)


def depths_of(parents, block_total):
    node = jnp.arange(block_total, dtype=jnp.int32)
    depths = jnp.zeros((block_total,), jnp.int32)
    link = (jnp.arange(block_total, dtype=jnp.int32)[None, :], parents[None, :])
    for _ in range(DEPTH - 1):
        above = jnp.sum(jnp.where(node[:, None] == link[0], link[1], 0), axis=1)
        node = jnp.where(node > 0, above, -1)
        depths = depths + (node >= 0).astype(jnp.int32)
    return depths


def rope_rows(depths):
    position = (depths[:, None] * BLOCK + jnp.arange(BLOCK, dtype=jnp.int32)).reshape(-1)
    frequency = jnp.exp(
        jnp.arange(HD // 2, dtype=jnp.float32) * (-2.0 * math.log(THETA) / HD)
    )
    angles = position.astype(jnp.float32)[:, None] * frequency[None, :]
    return jnp.cos(angles), jnp.sin(angles)


def rotate(rows, cosine, sine):
    heads = rows.reshape(rows.shape[0], -1, 2, HD // 2)
    lead, trail = heads[:, :, 0], heads[:, :, 1]
    c, s = cosine[:, None, :], sine[:, None, :]
    return jnp.stack([lead * c - trail * s, trail * c + lead * s], axis=2).reshape(rows.shape)


def shards(hidden, queries, key_weight, value_weight, parents, upstream):
    rows = hidden.shape[0]
    blocks = rows // BLOCK
    key_width = key_weight.shape[1]
    block_total = parents.shape[0]
    depths = lax.dynamic_slice_in_dim(
        depths_of(parents, block_total), lax.axis_index("ctx") * blocks, blocks, 0
    )
    cosine, sine = rope_rows(depths)
    features = lax.all_gather(hidden, "tp", axis=1, tiled=True)
    hidden_columns = lax.all_to_all(features, "ctx", split_axis=1, concat_axis=0, tiled=True)
    key_linear = jnp.dot(features, key_weight, preferred_element_type=jnp.float32)
    keys = rotate(key_linear, cosine, sine).astype(jnp.bfloat16)
    values = jnp.dot(features, value_weight, preferred_element_type=jnp.float32).astype(
        jnp.bfloat16
    )
    kv = lax.all_gather(jnp.concatenate([keys, values], axis=1), "ctx", axis=0, tiled=True)
    attention, query_grad, part = attention_call(parents, kv, queries, upstream, jnp.float32)
    own = lax.psum_scatter(part, "ctx", scatter_dimension=0, tiled=True)
    key_grad = rotate(own[:, :key_width], cosine, -sine).astype(jnp.bfloat16)
    value_grad = own[:, key_width:].astype(jnp.bfloat16)
    grads = lax.all_gather(
        jnp.concatenate([key_grad, value_grad], axis=1), "ctx", axis=0, tiled=True
    )
    weight_grads = lax.dot_general(
        hidden_columns, grads, (((0,), (0,)), ((), ())), preferred_element_type=jnp.float32
    )
    partial = dot_f32(key_grad, key_weight, 1, 1) + dot_f32(value_grad, value_weight, 1, 1)
    hidden_grad = lax.psum_scatter(
        partial.astype(jnp.bfloat16), "tp", scatter_dimension=1, tiled=True
    )
    return (
        attention,
        query_grad,
        hidden_grad,
        weight_grads[:, :key_width],
        weight_grads[:, key_width:],
    )


def solution(mesh):
    return jax.shard_map(
        shards,
        mesh=mesh,
        in_specs=(
            P("ctx", "tp"),
            P("ctx", "tp"),
            P(None, "tp"),
            P(None, "tp"),
            P(),
            P("ctx", "tp"),
        ),
        out_specs=(P("ctx", "tp"),) * 5,
        check_vma=False,
    )
```

time: 393 us -> 279 us (0.71); the launches traced: 386 us -> 279 us
  waiting for transfers between devices: 212 us -> 168 us
  local copies, waits for them, and re-layouts: 57.2 us -> 14.1 us
  matrix products: 31.5 us -> 14 us
  Pallas kernels: 0 us -> 17.4 us
  loops' own time: 17.2 us -> 0 us
    reduce_scatter x2, waiting for transfers between devices: 132 us -> 89.4 us  [the longest x1 51.5 us: shards(): own = lax.psum_scatter(part, 'ctx', scatter_dimension=0, tiled=True)]
    cond x27 -> x0, local copies, waits for them, and re-layouts: 17.5 us -> none
    dot_general x14 -> x3, matrix products: 25.2 us -> 7.73 us  [the longest x1 4.41 us: shards(): lax.dot_general(hidden_columns, grads, (((0,), (0,)), ((), ())), preferre...]
    pallas_call x0 -> x1, Pallas kernels: none -> 17.4 us  [attention_call(): pl.pallas_call(attend, name='attend', out_shape=(jax.ShapeDtypeStruct(que...]
    another operation x1 -> x0, loops' own time: 17.2 us -> none  [shards(): lax.switch(bucket, [partial(attend_slots, slot_count) for slot_count in b...]
    reshape x8 -> x0, local copies, waits for them, and re-layouts: 13.3 us -> none  [the longest x1 3.93 us: shards(): pair_grads = lax.psum_scatter(jnp.dot(selector, flat_grads, precision=HIG...]
    reduce_sum x2 -> x7, other arithmetic: 1.6 us -> 5.81 us  [depths_of(): above = jnp.sum(jnp.where(node[:, None] == link[0], link[1], 0), axis=1)]
  transfers between devices with their start and end apart: 5 -> 5, of which waited for: 4 -> 4; matrix products, arithmetic and copies ran while one was open for 5% -> 8% of each run, Pallas kernels for 0% -> 0%
where the time goes in v1:
time: 279 us
  waiting for transfers between devices  168 us (60%)
  blocking collectives  43.4 us (16%)
  Pallas kernels  17.4 us (6%)
  local copies, waits for them, and re-layouts  14.1 us (5%)
  matrix products  14 us (5%)
  between operations  13.9 us (5%)
  other arithmetic  7.88 us (3%)
    all_gather x1, waiting for transfers between devices, shards(): features = lax.all_gather(hidden, 'tp', axis=1, tiled=True)  51.7 us
    reduce_scatter x1, waiting for transfers between devices, shards(): own = lax.psum_scatter(part, 'ctx', scatter_dimension=0, tiled=True)  51.5 us
    all_to_all x1, blocking collectives, shards(): lax.all_to_all(features, 'ctx', split_axis=1, concat_axis=0, tiled=True)  43.4 us
    reduce_scatter x1, waiting for transfers between devices, shards(): lax.psum_scatter(partial.astype(jnp.bfloat16), 'tp', scatter_dimension=1,...  37.9 us
    all_gather x1, waiting for transfers between devices, shards(): lax.all_gather(jnp.concatenate([keys, values], axis=1), 'ctx', axis=0, ti...  26.8 us
    pallas_call x1, Pallas kernels, attention_call(): pl.pallas_call(attend, name='attend', out_shape=(jax.ShapeDtypeStruct(que...  17.4 us
    unnamed x9, local copies, waits for them, and re-layouts  6.51 us
    reduce_sum x7, other arithmetic, depths_of(): above = jnp.sum(jnp.where(node[:, None] == link[0], link[1], 0), axis=1)  5.81 us
  transfers between devices with their start and end apart: 5, of which 4 were waited for; matrix products, arithmetic and copies ran while one was open for 8% of the time, Pallas kernels for 0%

profile of v1, /device:TPU:0, one launch (start us, length us, event | category | flops | bytes accessed | tf_op | source)
XLA Modules:
  0.0 278.8 jit_solution(16555430898172776706)
XLA Ops:
  7.2 2.3 copy.30
  10.4 0.8 select_reduce_fusion.5
  11.3 0.8 select_reduce_fusion.4
  12.1 0.8 select_reduce_fusion.3
  13.0 0.8 select_reduce_fusion.2
  13.8 0.8 select_reduce_fusion.1
  16.0 51.7 %all-gather.4.cloned.1.call-done = bf16[256,5120]{0,1:T(8,128)(2,1)} async-done(((bf16[256,1280]{0,1:T(8,128)(2,1)}), bf16[256,5120]{0,1:T(8,128)(2,1)}) %all-gather.4.cloned.1.call-update) | async-done | bytes 2621456 | tf_op jit(solution)/shard_map/all_gather | solution.py:201
  67.7 2.9 %fusion.10 = f32[256,256]{0,1:T(8,128)S(1)} fusion(bf16[256,5120]{0,1:T(8,128)(2,1)} %all-gather.4.cloned.1.call-done, bf16[5120,256]{1,0:T(8,128)(2,1)S(1)} %copy-done), kind=kOutput, calls=%fused_computation.55 | convolution fusion | flops 671088640 | bytes 5505024 | tf_op jit(solution)/shard_map/dot_general | solution.py:203
  70.8 3.4 %convolution_convert_fusion = bf16[256,256]{1,0:T(8,128)(2,1)S(1)} fusion(bf16[256,5120]{0,1:T(8,128)(2,1)} %all-gather.4.cloned.1.call-done, bf16[5120,256]{1,0:T(8,128)(2,1)} %param.9), kind=kOutput, calls=%fused_computation.3 | convolution fusion | flops 671154176 | bytes 5373952 | tf_op jit(solution)/shard_map/dot_general | solution.py:205
  75.0 26.8 %all-gather.6.cloned.1.call-done.kv_ref = bf16[2048,512]{1,0:T(8,128)(2,1)} async-done(((bf16[256,512]{1,0:T(8,128)(2,1)}), bf16[2048,512]{1,0:T(8,128)(2,1)}) %all-gather.6.cloned.1.call-update) | async-done | bytes 2097168 | tf_op jit(solution)/shard_map/all_gather | solution.py:208
  101.7 17.4 %attend.1 = (bf16[256,1280]{1,0:T(8,128)(2,1)}, bf16[256,1280]{1,0:T(8,128)(2,1)}, f32[2048,512]{1,0:T(8,128)}) custom-call(s32[16]{0:T(128)} %parents_ref.1, bf16[2048,512]{1,0:T(8,128)(2,1)} %all-gather.6.cloned.1.call-done.kv_ref, bf16[256,1280]{1,0:T(8,128)(2,1)} %q_ref.1, bf16[256,1280]{1,0:T(8,128)(2,1)} %u_ref.1), custom_call_target="tpu_custom_call" | custom-call | tf_op jit(solution)/shard_map/attend/pallas_call | solution.py:147
  119.2 51.5 %reduce-scatter.3.cloned.1.call-done = f32[256,512]{1,0:T(8,128)} async-done(((f32[2048,512]{1,0:T(8,128)}), f32[256,512]{1,0:T(8,128)}) %reduce-scatter.3.cloned.1.call-update) | async-done | bytes 524304 | tf_op jit(solution)/shard_map/reduce_scatter | solution.py:210
  170.6 1.0 slice.35
  171.9 1.0 slice.50
  173.7 0.9 fusion.11
  174.7 0.9 copy-done.1
  175.5 2.4 fusion
  178.0 43.4 %all_to_all.19 = bf16[256,8,640]{0,2,1:T(8,128)(2,1)} all-to-all(bf16[256,8,640]{0,2,1:T(8,128)(2,1)} %bitcast.21), channel_id=1, replica_groups=mesh['ctx'=8,'tp'=4] {'ctx'}, dimensions={1} | all-to-all | bytes 5242880 | tf_op jit(solution)/shard_map/all_to_all | solution.py:202
  221.4 4.4 %copy.35 = bf16[8,256,640]{2,1,0:T(8,128)(2,1)} copy(bf16[8,256,640]{1,2,0:T(8,128)(2,1)} %bitcast.20) | data formatting | bytes 5242880 | tf_op jit(solution)/shard_map/all_to_all | solution.py:202
  225.8 4.4 %convolution_bitcast_fusion = f32[640,512]{0,1:T(8,128)S(1)} fusion(bf16[2048,512]{1,0:T(8,128)(2,1)} %all-gather.8.cloned.1.call-done, bf16[2048,640]{1,0:T(8,128)(2,1)} %bitcast.22), kind=kOutput, calls=%fused_computation.2 | convolution fusion | flops 1342177280 | bytes 6029312 | tf_op jit(solution)/shard_map/dot_general | solution.py:216
  230.2 0.9 fusion.8
  231.1 2.2 copy.37
  233.3 1.1 copy.36
  234.3 37.9 %reduce-scatter.5.cloned.1.call-done = bf16[256,1280]{1,0:T(8,128)(2,1)} async-done(((bf16[256,5120]{1,0:T(8,128)(2,1)}), bf16[256,1280]{1,0:T(8,128)(2,1)}) %reduce-scatter.5.cloned.1.call-update) | async-done | bytes 655376 | tf_op jit(solution)/shard_map/reduce_scatter | solution.py:220
  (38 shorter events, 4.4 us)
Async XLA Ops:
  7.2 60.5 %copy-start = (bf16[5120,256]{1,0:T(8,128)(2,1)S(1)}, bf16[5120,256]{1,0:T(8,128)(2,1)}, u32[]{:S(2)}) copy-start(bf16[5120,256]{1,0:T(8,128)(2,1)} %param.8) | copy-start | bytes 7864324
  7.2 60.5 %all-gather.4.cloned.1.call-start = ((), (), s32[]{:S(2)}) async-start(), calls=%async_computation.3 | async-start | bytes 3276800 | tf_op jit(solution)/shard_map/all_gather | solution.py:201
  9.6 92.2 %all-gather.6.cloned.1.call-start = ((), (), s32[]{:S(2)}) async-start(), calls=%async_computation.4 | async-start | bytes 2359296 | tf_op jit(solution)/shard_map/all_gather | solution.py:208
  74.9 95.7 %reduce-scatter.3.cloned.1.call-start = ((), (), s32[]{:S(2)}) async-start(), calls=%async_computation.5 | async-start | bytes 4718592 | tf_op jit(solution)/shard_map/reduce_scatter | solution.py:210
  119.1 106.6 %all-gather.8.cloned.1.call-start = ((), (), s32[]{:S(2)}) async-start(), calls=%async_computation.7 | async-start | bytes 2359296 | tf_op jit(solution)/shard_map/all_gather | solution.py:213
  173.6 1.0 copy-start.2
  173.6 98.6 %reduce-scatter.5.cloned.1.call-start = ((), (), s32[]{:S(2)}) async-start(), calls=%async_computation.6 | async-start | bytes 3276800 | tf_op jit(solution)/shard_map/reduce_scatter | solution.py:220
  173.7 1.9 copy-start.1
Sparse Core Ops, SparseCore 0:
  10.2 57.4 all-gather.3
  75.0 26.6 all-gather.5
  119.2 51.3 reduce-scatter.2
  173.7 43.3 all-gather.7
  220.0 52.1 reduce-scatter.4

commit v2 on v1

--- a/solution.py
+++ b/solution.py
@@ -1,3 +1,4 @@
+from functools import partial
 import math
 
 import jax
@@ -162,76 +163,569 @@
     )(parents, kv, queries, upstream)
 
 
-def depths_of(parents, block_total):
-    node = jnp.arange(block_total, dtype=jnp.int32)
-    depths = jnp.zeros((block_total,), jnp.int32)
-    link = (jnp.arange(block_total, dtype=jnp.int32)[None, :], parents[None, :])
-    for _ in range(DEPTH - 1):
-        above = jnp.sum(jnp.where(node[:, None] == link[0], link[1], 0), axis=1)
-        node = jnp.where(node > 0, above, -1)
-        depths = depths + (node >= 0).astype(jnp.int32)
-    return depths
-
-
-def rope_rows(depths):
-    position = (depths[:, None] * BLOCK + jnp.arange(BLOCK, dtype=jnp.int32)).reshape(-1)
-    frequency = jnp.exp(
-        jnp.arange(HD // 2, dtype=jnp.float32) * (-2.0 * math.log(THETA) / HD)
-    )
-    angles = position.astype(jnp.float32)[:, None] * frequency[None, :]
-    return jnp.cos(angles), jnp.sin(angles)
-
-
-def rotate(rows, cosine, sine):
-    heads = rows.reshape(rows.shape[0], -1, 2, HD // 2)
-    lead, trail = heads[:, :, 0], heads[:, :, 1]
-    c, s = cosine[:, None, :], sine[:, None, :]
-    return jnp.stack([lead * c - trail * s, trail * c + lead * s], axis=2).reshape(rows.shape)
-
-
-def shards(hidden, queries, key_weight, value_weight, parents, upstream):
-    rows = hidden.shape[0]
+def remote(src, dst, send_sem, recv_sem, ctx, tp):
+    return pltpu.make_async_remote_copy(
+        src_ref=src,
+        dst_ref=dst,
+        send_sem=send_sem,
+        recv_sem=recv_sem,
+        device_id=(ctx, tp),
+        device_id_type=MESH,
+    )
+
+
+def greet(devices, count):
+    barrier = pltpu.get_barrier_semaphore()
+    for ctx, tp, valid in devices:
+        if valid is None:
+            pl.semaphore_signal(barrier, inc=1, device_id=(ctx, tp), device_id_type=MESH)
+        else:
+
+            @pl.when(valid)
+            def _():
+                pl.semaphore_signal(barrier, inc=1, device_id=(ctx, tp), device_id_type=MESH)
+
+    pl.semaphore_wait(barrier, count)
+
+
+class PlaneGather:
+    def __init__(self, buf, chips, send, recv, sib_send, sib_recv):
+        me, tp = lax.axis_index("ctx"), lax.axis_index("tp")
+        self.buf, self.chips = buf, chips
+        self.sems = (send, recv, sib_send, sib_recv)
+        self.me, self.tp = me, tp
+        self.chip, self.core = me // 2, me % 2
+
+    def holder(self, offset):
+        return (self.chip + self.chips - offset) % self.chips * 2
+
+    def out_copy(self, offset):
+        peer = (self.chip + offset) % self.chips * 2 + self.core
+        slot = self.buf.at[self.me]
+        return remote(
+            slot, slot, self.sems[0].at[offset], self.sems[1].at[offset], peer, self.tp
+        )
+
+    def sib_copy(self, offset):
+        slot = self.buf.at[self.holder(offset) + self.core]
+        return remote(
+            slot,
+            slot,
+            self.sems[2].at[offset],
+            self.sems[3].at[offset],
+            self.holder(0) + 1 - self.core,
+            self.tp,
+        )
+
+    def start(self):
+        for offset in range(1, self.chips):
+            self.out_copy(offset).start()
+        self.sib_copy(0).start()
+
+    def arrive(self, offset):
+        self.out_copy(offset).wait_recv()
+        self.sib_copy(offset).start()
+        return self.holder(offset) + self.core
+
+    def arrive_sibling(self, offset):
+        self.sib_copy(offset).wait_recv()
+        return self.holder(offset) + 1 - self.core
+
+    def drain(self):
+        for offset in range(self.chips):
+            if offset:
+                self.out_copy(offset).wait_send()
+            self.sib_copy(offset).wait_send()
+
+
+class Line:
+    def __init__(self, slot_of, size, sems):
+        self.ctx, self.tp = lax.axis_index("ctx"), lax.axis_index("tp")
+        self.slot_of, self.size, self.sems = slot_of, size, sems
+
+    def send(self, way, k):
+        source = self.tp - k if way == 0 else self.tp + k
+        valid = (
+            (source >= 0) & (self.tp < self.size - 1)
+            if way == 0
+            else (source < self.size) & (self.tp > 0)
+        )
+        slot = self.slot_of(source)
+        target = self.tp + 1 if way == 0 else self.tp - 1
+        return valid, remote(
+            slot, slot, self.sems[0].at[way, k], self.sems[1].at[way, k], self.ctx, target
+        )
+
+    def start(self, k):
+        for way in range(2):
+            valid, copy = self.send(way, k)
+
+            @pl.when(valid)
+            def _(copy=copy):
+                copy.start()
+
+    def arrive(self, k, then):
+        for way in range(2):
+            source = self.tp - 1 - k if way == 0 else self.tp + 1 + k
+            valid = source >= 0 if way == 0 else source < self.size
+            slot = self.slot_of(source)
+
+            @pl.when(valid)
+            def _(way=way, source=source, slot=slot):
+                remote(
+                    slot, slot, self.sems[0].at[way, k], self.sems[1].at[way, k], self.ctx, self.tp
+                ).wait_recv()
+                if k + 1 < self.size - 1:
+                    on, copy = self.send(way, k + 1)
+
+                    @pl.when(on)
+                    def _():
+                        copy.start()
+
+                then(way, source)
+
+    def drain(self):
+        for k in range(self.size - 1):
+            for way in range(2):
+                valid, copy = self.send(way, k)
+
+                @pl.when(valid)
+                def _(copy=copy):
+                    copy.wait_send()
+
+
+def gather_kernel(
+    ctx_size,
+    tp_size,
+    merged,
+    parents_ref,
+    hid_ref,
+    kw_ref,
+    vw_ref,
+    kw_any,
+    vw_any,
+    base_ref,
+    near_ref,
+    kv_ref,
+    cols_ref,
+    piece_ref,
+    cos_ref,
+    sin_ref,
+    feat,
+    acc,
+    line_send,
+    line_recv,
+    kv_send,
+    kv_recv,
+    sib_send,
+    sib_recv,
+    col_send,
+    col_recv,
+    w_send,
+    w_recv,
+):
+    me, tp = lax.axis_index("ctx"), lax.axis_index("tp")
+    width, rows = hid_ref.shape
+    half = width // 2
+    key_width = kw_ref.shape[1]
     blocks = rows // BLOCK
-    key_width = key_weight.shape[1]
-    block_total = parents.shape[0]
-    depths = lax.dynamic_slice_in_dim(
-        depths_of(parents, block_total), lax.axis_index("ctx") * blocks, blocks, 0
-    )
-    cosine, sine = rope_rows(depths)
-    features = lax.all_gather(hidden, "tp", axis=1, tiled=True)
-    hidden_columns = lax.all_to_all(features, "ctx", split_axis=1, concat_axis=0, tiled=True)
-    key_linear = jnp.dot(features, key_weight, preferred_element_type=jnp.float32)
-    keys = rotate(key_linear, cosine, sine).astype(jnp.bfloat16)
-    values = jnp.dot(features, value_weight, preferred_element_type=jnp.float32).astype(
-        jnp.bfloat16
-    )
-    kv = lax.all_gather(jnp.concatenate([keys, values], axis=1), "ctx", axis=0, tiled=True)
-    attention, query_grad, part = attention_call(parents, kv, queries, upstream, jnp.float32)
-    own = lax.psum_scatter(part, "ctx", scatter_dimension=0, tiled=True)
-    key_grad = rotate(own[:, :key_width], cosine, -sine).astype(jnp.bfloat16)
-    value_grad = own[:, key_width:].astype(jnp.bfloat16)
-    grads = lax.all_gather(
-        jnp.concatenate([key_grad, value_grad], axis=1), "ctx", axis=0, tiled=True
-    )
-    weight_grads = lax.dot_general(
-        hidden_columns, grads, (((0,), (0,)), ((), ())), preferred_element_type=jnp.float32
-    )
-    partial = dot_f32(key_grad, key_weight, 1, 1) + dot_f32(value_grad, value_weight, 1, 1)
-    hidden_grad = lax.psum_scatter(
-        partial.astype(jnp.bfloat16), "tp", scatter_dimension=1, tiled=True
-    )
+    col_rows = cols_ref.shape[1]
+    per_half = half // col_rows
+    greet(
+        [((me + o) % ctx_size, tp, None) for o in range(1, ctx_size)]
+        + [(me, (tp + o) % tp_size, None) for o in range(1, tp_size)],
+        ctx_size + tp_size - 2,
+    )
+    for j in range(2):
+        feat[tp, j] = hid_ref[j * half : (j + 1) * half, :]
+    lines = [
+        Line(lambda s, j=j: feat.at[s, j], tp_size, (line_send.at[j], line_recv.at[j]))
+        for j in range(2)
+    ]
+    lines[0].start(0)
+
+    def col_copy(source, j, i):
+        dest = (source * 2 + j) * per_half + i
+        offset = (dest + ctx_size - me) % ctx_size
+        return dest, remote(
+            feat.at[source, j, pl.ds(i * col_rows, col_rows), :],
+            cols_ref.at[me],
+            col_send.at[offset],
+            col_recv.at[offset],
+            dest,
+            tp,
+        )
+
+    def share(source, j):
+        for i in range(per_half):
+            dest, copy = col_copy(source, j, i)
+
+            @pl.when(dest != me)
+            def _(copy=copy):
+                copy.start()
+
+            @pl.when(dest == me)
+            def _(i=i):
+                cols_ref[me] = feat[source, j, i * col_rows : (i + 1) * col_rows, :]
+
+    def project(source, j):
+        at = pl.ds(pl.multiple_of(source * width + j * half, 128), half)
+        block = feat[source, j]
+        acc[:, :key_width] += dot_f32(block, kw_ref[at, :], 0, 0)
+        acc[:, key_width:] += dot_f32(block, vw_ref[at, :], 0, 0)
+
+    acc[...] = jnp.zeros_like(acc)
+    lines[1].start(0)
+    for j in range(2):
+        share(tp, j)
+
+    first = me * blocks
+    lane = lax.broadcasted_iota(jnp.int32, (BLOCK, HD), 1)
+    sign = jnp.where(lane < HD // 2, -1.0, 1.0)
+    for b in range(blocks):
+        depth, _ = walk(parents_ref, first + b)
+        pick = lax.broadcasted_iota(jnp.int32, (DEPTH, HD), 0) == depth
+        base_cos = jnp.sum(jnp.where(pick, base_ref[0], 0.0), axis=0, keepdims=True)
+        base_sin = jnp.sum(jnp.where(pick, base_ref[1], 0.0), axis=0, keepdims=True)
+        at = slice(b * BLOCK, (b + 1) * BLOCK)
+        cos_ref[at, :] = base_cos * near_ref[0] - base_sin * near_ref[1]
+        sin_ref[at, :] = (base_sin * near_ref[0] + base_cos * near_ref[1]) * sign
+
+    for j in range(2):
+        project(tp, j)
+    late = []
+    for j in range(2):
+        for k in range(tp_size - 1):
+            last = j == 1 and k == tp_size - 2
+
+            def then(way, source, j=j, last=last):
+                if not last:
+                    share(source, j)
+                project(source, j)
+
+            lines[j].arrive(k, then)
+
+    def piece_copy(offset, matrix):
+        target = (tp + offset) % tp_size
+        return remote(
+            (kw_any, vw_any)[matrix].at[target, me],
+            piece_ref.at[tp_size - 1 - offset, matrix],
+            w_send.at[offset, matrix],
+            w_recv.at[offset, matrix],
+            me,
+            target,
+        )
+
+    for offset in range(1, tp_size):
+        for matrix in range(2):
+            piece_copy(offset, matrix).start()
+
+    cosine, sine = cos_ref[...], sin_ref[...]
+    for g in range(key_width // HD):
+        at = slice(g * HD, (g + 1) * HD)
+        x = acc[:, at]
+        kv_ref[me, :, at] = (x * cosine + pltpu.roll(x, HD // 2, 1) * sine).astype(jnp.bfloat16)
+    kv_ref[me, :, key_width:] = acc[:, key_width:].astype(jnp.bfloat16)
+    gather = PlaneGather(kv_ref, ctx_size // 2, kv_send, kv_recv, sib_send, sib_recv)
+    gather.start()
+    for offset in range(1, ctx_size // 2):
+        gather.arrive(offset)
+    k = tp_size - 2
+    for way in range(2):
+        source = tp - 1 - k if way == 0 else tp + 1 + k
+        valid = source >= 0 if way == 0 else source < tp_size
+
+        @pl.when(valid)
+        def _(source=source):
+            share(source, 1)
+
+    for offset in range(ctx_size // 2):
+        gather.arrive_sibling(offset)
+    if merged is not None:
+        merged()
+    for offset in range(1, ctx_size):
+        remote(
+            cols_ref.at[(me + ctx_size - offset) % ctx_size],
+            cols_ref.at[(me + ctx_size - offset) % ctx_size],
+            col_send.at[offset],
+            col_recv.at[offset],
+            me,
+            tp,
+        ).wait()
+    for offset in range(1, tp_size):
+        for matrix in range(2):
+            piece_copy(offset, matrix).wait()
+    gather.drain()
+    for line in lines:
+        line.drain()
+
+
+def grads_kernel(
+    ctx_size,
+    tp_size,
+    part_ref,
+    cos_ref,
+    sin_ref,
+    cols_ref,
+    piece_ref,
+    kw_ref,
+    vw_ref,
+    hg_ref,
+    kwg_ref,
+    vwg_ref,
+    total,
+    sib_buf,
+    chip_buf,
+    rs_buf,
+    gbuf,
+    zbuf,
+    wall,
+    hg_acc,
+    a_send,
+    a_recv,
+    b_send,
+    b_recv,
+    g_send,
+    g_recv,
+    gs_send,
+    gs_recv,
+    w_send,
+    w_recv,
+    ws_send,
+    ws_recv,
+    line_send,
+    line_recv,
+):
+    me, tp = lax.axis_index("ctx"), lax.axis_index("tp")
+    chips = ctx_size // 2
+    chip, core = me // 2, me % 2
+    rows, pair_width = total.shape
+    key_width = pair_width // 2
+    up, down = tp < tp_size - 1, tp > 0
+    sibling = chip * 2 + 1 - core
+    greet(
+        [((chip + o) % chips * 2 + core, tp, None) for o in range(1, chips)]
+        + [(sibling, tp, None)]
+        + [(me, jnp.minimum(tp + 1, tp_size - 1), up), (me, jnp.maximum(tp - 1, 0), down)],
+        chips + jnp.where(up, 1, 0) + jnp.where(down, 1, 0),
+    )
+
+    def sib_copy(offset):
+        target = (chip + offset) % chips
+        return remote(
+            part_ref.at[target * 2 + 1 - core],
+            sib_buf.at[offset],
+            a_send.at[offset],
+            a_recv.at[offset],
+            sibling,
+            tp,
+        )
+
+    def chip_copy(offset):
+        target = (chip + offset) % chips
+        return remote(
+            chip_buf.at[offset],
+            rs_buf.at[offset],
+            b_send.at[offset],
+            b_recv.at[offset],
+            target * 2 + core,
+            tp,
+        )
+
+    order = list(range(1, chips)) + [0]
+    for offset in order:
+        sib_copy(offset).start()
+    wall[me] = piece_ref[...]
+    for offset in order:
+        sib_copy(offset).wait_recv()
+        own = part_ref[(chip + offset) % chips * 2 + core]
+        both = own.astype(jnp.float32) + sib_buf[offset].astype(jnp.float32)
+        if offset:
+            chip_buf[offset] = both.astype(jnp.bfloat16)
+            chip_copy(offset).start()
+        else:
+            total[...] = both
+    weights = PlaneGather(wall, chips, w_send, w_recv, ws_send, ws_recv)
+    for offset in range(1, chips):
+        chip_copy(offset).wait_recv()
+        total[...] += rs_buf[offset].astype(jnp.float32)
+    cosine, sine = cos_ref[...], sin_ref[...]
+    for g in range(key_width // HD):
+        at = slice(g * HD, (g + 1) * HD)
+        x = total[:, at]
+        zbuf[tp, :, at] = (x * cosine - pltpu.roll(x, HD // 2, 1) * sine).astype(jnp.bfloat16)
+    zbuf[tp, :, key_width:] = total[:, key_width:].astype(jnp.bfloat16)
+    gbuf[me] = zbuf[tp]
+    line = Line(lambda s: zbuf.at[s], tp_size, (line_send, line_recv))
+    line.start(0)
+    grads = PlaneGather(gbuf, chips, g_send, g_recv, gs_send, gs_recv)
+    grads.start()
+    weights.start()
+
+    def weight_grad(source, fresh=False):
+        left = cols_ref[source]
+        key_part = dot_f32(left, gbuf[source, :, :key_width], 1, 0)
+        value_part = dot_f32(left, gbuf[source, :, key_width:], 1, 0)
+        if fresh:
+            kwg_ref[...] = key_part
+            vwg_ref[...] = value_part
+        else:
+            kwg_ref[...] += key_part
+            vwg_ref[...] += value_part
+
+    def hidden_grad(source, key_rows, value_rows):
+        part = dot_f32(zbuf[source, :, :key_width], key_rows, 1, 1) + dot_f32(
+            zbuf[source, :, key_width:], value_rows, 1, 1
+        )
+        return part.astype(jnp.bfloat16).astype(jnp.float32)
+
+    weight_grad(me, True)
+    hg_acc[...] = hidden_grad(tp, kw_ref[...], vw_ref[...])
+    line.arrive(0, lambda way, source: None)
+    for offset in range(1, chips):
+        weight_grad(grads.arrive(offset))
+        if offset < tp_size - 1:
+            line.arrive(offset, lambda way, source: None)
+    for k in range(chips, tp_size - 1):
+        line.arrive(k, lambda way, source: None)
+    for offset in range(1, chips):
+        weights.arrive(offset)
+    for offset in range(chips):
+        weight_grad(grads.arrive_sibling(offset))
+    for offset in range(chips):
+        weights.arrive_sibling(offset)
+
+    def rows_of(j, matrix):
+        pieces = [wall[c, j, matrix] for c in range(ctx_size)]
+        if wall.shape[3] % 16:
+            pieces = [piece.astype(jnp.float32) for piece in pieces]
+        return jnp.concatenate(pieces, axis=0).astype(jnp.bfloat16)
+
+    for j in range(tp_size - 1):
+        source = (tp + 1 + j) % tp_size
+        hg_acc[...] += hidden_grad(source, rows_of(j, 0), rows_of(j, 1))
+    hg_ref[...] = hg_acc[...].astype(jnp.bfloat16)
+    for offset in range(chips):
+        sib_copy(offset).wait_send()
+        if offset:
+            chip_copy(offset).wait_send()
+    grads.drain()
+    weights.drain()
+    line.drain()
+
+
+def rope_tables():
+    lane = jnp.arange(HD, dtype=jnp.int32) % (HD // 2)
+    frequency = jnp.exp(lane.astype(jnp.float32) * (-2.0 * math.log(THETA) / HD))
+    base = (jnp.arange(DEPTH, dtype=jnp.int32) * BLOCK).astype(jnp.float32)[:, None] * frequency
+    near = jnp.arange(BLOCK, dtype=jnp.int32).astype(jnp.float32)[:, None] * frequency
     return (
-        attention,
-        query_grad,
-        hidden_grad,
-        weight_grads[:, :key_width],
-        weight_grads[:, key_width:],
-    )
+        jnp.stack([jnp.cos(base), jnp.sin(base)]),
+        jnp.stack([jnp.cos(near), jnp.sin(near)]),
+    )
+
+
+def shards(ctx_size, tp_size, hidden, queries, key_weight, value_weight, parents, upstream):
+    rows, width = hidden.shape
+    depth_rows, key_width = key_weight.shape
+    pair_width = 2 * key_width
+    col_rows = depth_rows // ctx_size
+    piece_rows = width // ctx_size
+    chips = ctx_size // 2
+    vmem = pl.BlockSpec(memory_space=pltpu.VMEM)
+    anywhere = pl.BlockSpec(memory_space=pl.ANY)
+    smem = pl.BlockSpec(memory_space=pltpu.SMEM)
+    bf16, f32 = jnp.bfloat16, jnp.float32
+    dma = pltpu.SemaphoreType.DMA
+    base, near = rope_tables()
+    split = (tp_size, ctx_size, piece_rows, key_width)
+
+    def params(collective_id):
+        return pltpu.CompilerParams(
+            collective_id=collective_id, has_side_effects=True, vmem_limit_bytes=VMEM_LIMIT
+        )
+
+    kv, cols, pieces, cosine, sine = pl.pallas_call(
+        partial(gather_kernel, ctx_size, tp_size, None),
+        name="gather_keys_values",
+        out_shape=(
+            jax.ShapeDtypeStruct((ctx_size, rows, pair_width), bf16),
+            jax.ShapeDtypeStruct((ctx_size, col_rows, rows), bf16),
+            jax.ShapeDtypeStruct((tp_size - 1, 2, piece_rows, key_width), bf16),
+            jax.ShapeDtypeStruct((rows, HD), f32),
+            jax.ShapeDtypeStruct((rows, HD), f32),
+        ),
+        in_specs=[smem, vmem, vmem, vmem, anywhere, anywhere, vmem, vmem],
+        out_specs=(vmem,) * 5,
+        scratch_shapes=[
+            pltpu.VMEM((tp_size, 2, width // 2, rows), bf16),
+            pltpu.VMEM((rows, pair_width), f32),
+            dma((2, 2, tp_size - 1)),
+            dma((2, 2, tp_size - 1)),
+            dma((chips,)),
+            dma((chips,)),
+            dma((chips,)),
+            dma((chips,)),
+            dma((ctx_size,)),
+            dma((ctx_size,)),
+            dma((tp_size, 2)),
+            dma((tp_size, 2)),
+        ],
+        compiler_params=params(1),
+    )(
+        parents,
+        hidden.T,
+        key_weight,
+        value_weight,
+        key_weight.reshape(split),
+        value_weight.reshape(split),
+        base,
+        near,
+    )
+    attention, query_grad, part = attention_call(
+        parents, kv.reshape(ctx_size * rows, pair_width), queries, upstream, bf16
+    )
+    first = lax.axis_index("tp") * width
+    kw_own = lax.dynamic_slice_in_dim(key_weight, first, width, 0)
+    vw_own = lax.dynamic_slice_in_dim(value_weight, first, width, 0)
+    hidden_grad, key_weight_grad, value_weight_grad = pl.pallas_call(
+        partial(grads_kernel, ctx_size, tp_size),
+        name="sum_grads",
+        out_shape=(
+            jax.ShapeDtypeStruct(hidden.shape, bf16),
+            jax.ShapeDtypeStruct((col_rows, key_width), f32),
+            jax.ShapeDtypeStruct((col_rows, key_width), f32),
+        ),
+        in_specs=[vmem] * 7,
+        out_specs=(vmem,) * 3,
+        scratch_shapes=[
+            pltpu.VMEM((rows, pair_width), f32),
+            pltpu.VMEM((chips, rows, pair_width), bf16),
+            pltpu.VMEM((chips, rows, pair_width), bf16),
+            pltpu.VMEM((chips, rows, pair_width), bf16),
+            pltpu.VMEM((ctx_size, rows, pair_width), bf16),
+            pltpu.VMEM((tp_size, rows, pair_width), bf16),
+            pltpu.VMEM((ctx_size, tp_size - 1, 2, piece_rows, key_width), bf16),
+            pltpu.VMEM((rows, width), f32),
+        ]
+        + [dma((chips,))] * 12
+        + [dma((2, tp_size - 1))] * 2,
+        compiler_params=params(2),
+    )(
+        part.reshape(ctx_size, rows, pair_width),
+        cosine,
+        sine,
+        cols,
+        pieces,
+        kw_own,
+        vw_own,
+    )
+    return attention, query_grad, hidden_grad, key_weight_grad, value_weight_grad
 
 
 def solution(mesh):
     return jax.shard_map(
-        shards,
+        partial(shards, mesh.shape["ctx"], mesh.shape["tp"]),
         mesh=mesh,
         in_specs=(
             P("ctx", "tp"),

time: 279 us -> 173 us (0.62)
  waiting for transfers between devices: 168 us -> 0 us
  Pallas kernels: 17.4 us -> 161 us
  blocking collectives: 43.4 us -> 0 us
  matrix products: 14 us -> 0 us
  between operations: 13.9 us -> 0.67 us
  other arithmetic: 7.88 us -> 1.71 us
  local copies, waits for them, and re-layouts: 14.1 us -> 9.42 us
    pallas_call x0 -> x2, Pallas kernels: none -> 144 us  [the longest x1 78.4 us: shards(): pl.pallas_call(partial(gather_kernel, ctx_size, tp_size, None), name='gat...]
    reduce_scatter x2 -> x0, waiting for transfers between devices: 89.4 us -> none  [the longest x1 51.5 us: shards(): own = lax.psum_scatter(part, 'ctx', scatter_dimension=0, tiled=True)]
    all_gather x3 -> x0, waiting for transfers between devices: 78.5 us -> none  [the longest x1 51.7 us: shards(): features = lax.all_gather(hidden, 'tp', axis=1, tiled=True)]
    all_to_all x1 -> x0, blocking collectives: 43.4 us -> none  [shards(): lax.all_to_all(features, 'ctx', split_axis=1, concat_axis=0, tiled=True)]
    dot_general x5 -> x0, matrix products: 14 us -> none  [the longest x1 4.41 us: shards(): lax.dot_general(hidden_columns, grads, (((0,), (0,)), ((), ())), preferre...]
    reduce_sum x7 -> x0, other arithmetic: 5.81 us -> none  [depths_of(): above = jnp.sum(jnp.where(node[:, None] == link[0], link[1], 0), axis=1)]
    all_to_all x1 -> x0, local copies, waits for them, and re-layouts: 4.38 us -> none  [shards(): lax.all_to_all(features, 'ctx', split_axis=1, concat_axis=0, tiled=True)]
    slice x4 -> x0, local copies, waits for them, and re-layouts: 2.98 us -> none  [the longest x2 1.1 us: shards(): key_grad = rotate(own[:, :key_width], cosine, -sine).astype(jnp.bfloat16)]
  transfers between devices with their start and end apart: 5 -> 0, of which waited for: 4 -> 0; matrix products, arithmetic and copies ran while one was open for 8% -> 0% of each run, Pallas kernels for 0% -> 0%
where the time goes in v2:
time: 173 us; the launch traced here: 172 us
  Pallas kernels  161 us (93%)
  local copies, waits for them, and re-layouts  9.42 us (5%)
    pallas_call x1, Pallas kernels, shards(): pl.pallas_call(partial(gather_kernel, ctx_size, tp_size, None), name='gat...  78.4 us
    pallas_call x1, Pallas kernels, shards(): pl.pallas_call(partial(grads_kernel, ctx_size, tp_size), name='sum_grads'...  65.7 us
    pallas_call x1, Pallas kernels, attention_call(): pl.pallas_call(attend, name='attend', out_shape=(jax.ShapeDtypeStruct(que...  16.6 us
    unnamed x6, local copies, waits for them, and re-layouts  7 us

profile of v2, /device:TPU:0, one launch (start us, length us, event | category | flops | bytes accessed | tf_op | source)
XLA Modules:
  0.0 172.5 jit_solution(15436790232252952255)
XLA Ops:
  0.6 2.2 %copy.11 = bf16[256,1280]{0,1:T(8,128)(2,1)} copy(bf16[256,1280]{1,0:T(8,128)(2,1)} %param.6) | data formatting | bytes 1310720 | tf_op args[0]
  2.8 0.1 multiply_cosine_fusion.1
  2.9 0.6 pad_maximum_fusion.1.base_ref
  3.5 0.3 multiply_cosine_fusion
  3.8 0.7 pad_maximum_fusion.near_ref
  4.5 78.4 %gather_keys_values.1 = (bf16[8,256,512]{2,1,0:T(8,128)(2,1)}, bf16[8,640,256]{2,1,0:T(8,128)(2,1)}, bf16[3,2,160,256]{3,2,1,0:T(8,128)(2,1)}, f32[256,128]{1,0:T(8,128)}, f32[256,128]{1,0:T(8,128)}) custom-call(s32[16]{0:T(128)} %parents_ref.3, bf16[1280,256]{1,0:T(8,128)(2,1)} %bitcast.7, bf16[5120,256]{1,0:T(8,128)(2,1)} %kw_ref.1, ...), custom_call_target="tpu_custom_call" | custom-call | tf_op jit(solution)/shard_map/gather_keys_values/pallas_call | solution.py:648
  82.9 16.6 %attend.1 = (bf16[256,1280]{1,0:T(8,128)(2,1)}, bf16[256,1280]{1,0:T(8,128)(2,1)}, bf16[2048,512]{1,0:T(8,128)(2,1)}) custom-call(s32[16]{0:T(128)} %parents_ref.3, bf16[2048,512]{1,0:T(8,128)(2,1)} %bitcast.9, bf16[256,1280]{1,0:T(8,128)(2,1)} %q_ref.1, bf16[256,1280]{1,0:T(8,128)(2,1)} %u_ref.1), custom_call_target="tpu_custom_call" | custom-call | tf_op jit(solution)/shard_map/attend/pallas_call | solution.py:148
  99.5 2.4 %constant_dynamic-slice_fusion = (bf16[1280,256]{1,0:T(8,128)(2,1)}, bf16[1280,256]{1,0:T(8,128)(2,1)}) fusion(bf16[5120,256]{1,0:T(8,128)(2,1)} %vw_ref.1, s32[]{:T(128)S(6)} %select_n.22, bf16[5120,256]{1,0:T(8,128)(2,1)} %kw_ref.1), kind=kLoop, calls=%fused_computation.11 | loop fusion | bytes 2621444 | tf_op jit(solution)/shard_map/dynamic_slice | solution.py:690
  101.9 65.7 %sum_grads.1 = (bf16[256,1280]{1,0:T(8,128)(2,1)}, f32[640,256]{1,0:T(8,128)}, f32[640,256]{1,0:T(8,128)}) custom-call(bf16[8,256,512]{2,1,0:T(8,128)(2,1)} %bitcast.8, f32[256,128]{1,0:T(8,128)} %get-tuple-element.20.cos_ref, f32[256,128]{1,0:T(8,128)} %get-tuple-element.21.sin_ref, bf16[8,640,256]{2,1,0:T(8,128)(2,1)} %get-tuple-element.22.cols_ref, ...), custom_call_target="tpu_custom_call" | custom-call | tf_op jit(solution)/shard_map/sum_grads/pallas_call | solution.py:691
  167.6 0.0 copy-start
  167.6 2.0 %copy.15 = bf16[256,1280]{1,0:T(8,128)(2,1)} copy(bf16[256,1280]{1,0:T(8,128)(2,1)} %get-tuple-element.40) | data formatting | bytes 1310720
  169.6 2.0 %copy.16 = f32[640,256]{1,0:T(8,128)} copy(f32[640,256]{1,0:T(8,128)} %get-tuple-element.41) | data formatting | bytes 1310720
  171.6 0.0 copy-done
  171.6 0.8 copy.17
  (3 shorter events, 0.0 us)
Async XLA Ops:
  167.6 4.0 %copy-start = (f32[640,256]{1,0:T(8,128)S(1)}, f32[640,256]{1,0:T(8,128)}, u32[]{:S(2)}) copy-start(f32[640,256]{1,0:T(8,128)} %get-tuple-element.42) | copy-start | bytes 1966084

commit v3 on v2

v3 whole, which is shorter than its diff:
```python
from functools import partial
import math

import jax
import jax.numpy as jnp
from jax import lax
from jax.experimental import pallas as pl
from jax.experimental.pallas import tpu as pltpu
from jax.sharding import PartitionSpec as P

HD = 128
BLOCK = 128
DEPTH = 8
THETA = 1000000.0
NEGATIVE = -1e30
VMEM_LIMIT = 56 * 1024 * 1024
MESH = pl.DeviceIdType.MESH


def walk(parents_ref, block):
    chain = [block]
    for _ in range(DEPTH - 1):
        last = chain[-1]
        above = parents_ref[jnp.maximum(last, 0)]
        chain.append(jnp.where(last > 0, above, -1))
    depth = jnp.int32(0)
    for node in chain[1:]:
        depth = depth + jnp.where(node >= 0, 1, 0)
    path = []
    for level in range(DEPTH):
        found = jnp.int32(0)
        for hop in range(DEPTH):
            found = found + jnp.where(depth - hop == level, chain[hop], 0)
        path.append(found)
    return depth, path


def dot_f32(left, right, left_dim, right_dim):
    return lax.dot_general(
        left, right, (((left_dim,), (right_dim,)), ((), ())), preferred_element_type=jnp.float32
    )


def attend(parents_ref, kv_ref, q_ref, u_ref, att_ref, qg_ref, s_ref, grads_ref, release):
    rows, width = q_ref.shape
    blocks = rows // BLOCK
    pair_width = kv_ref.shape[2]
    key_width = pair_width // 2
    key_heads = key_width // HD
    groups = width // key_width
    lanes = groups * BLOCK
    step = 2 * BLOCK
    steps = DEPTH // 2
    scale = 1.0 / math.sqrt(HD)
    first = lax.axis_index("ctx") * blocks

    def one_block(b, carry):
        depth, path = walk(parents_ref, first + b)
        row0 = pl.multiple_of(b * BLOCK, BLOCK)
        here = pl.ds(row0, BLOCK)
        key_row = lax.broadcasted_iota(jnp.int32, (step, lanes), 0)
        query_row = lax.broadcasted_iota(jnp.int32, (step, lanes), 1) % BLOCK
        limit = depth * BLOCK + query_row - key_row
        for g in range(key_heads):
            def head_cols(h):
                return slice((g * groups + h) * HD, (g * groups + h + 1) * HD)

            key_cols = slice(g * HD, (g + 1) * HD)
            value_cols = slice(key_width + g * HD, key_width + (g + 1) * HD)
            q = jnp.concatenate([q_ref[here, head_cols(h)] for h in range(groups)], axis=0)
            u = jnp.concatenate([u_ref[here, head_cols(h)] for h in range(groups)], axis=0)
            u_t = u.astype(jnp.float32).T

            def pair(p, cols):
                return jnp.concatenate(
                    [
                        kv_ref[path[2 * p + i], :, cols] for i in range(2)
                    ],
                    axis=0,
                )

            top = jnp.full((1, lanes), NEGATIVE, jnp.float32)
            for p in range(steps):
                s = dot_f32(pair(p, key_cols), q, 1, 1) * scale
                s = jnp.where(limit >= p * step, s, NEGATIVE)
                s_ref[p] = s
                top = jnp.maximum(top, jnp.max(s, axis=0, keepdims=True))
            totals = jnp.zeros((1, lanes), jnp.float32)
            mixed = jnp.zeros((HD, lanes), jnp.float32)
            for p in range(steps):
                w = jnp.exp(s_ref[p] - top)
                s_ref[p] = w
                totals = totals + jnp.sum(w, axis=0, keepdims=True)
                mixed = mixed + dot_f32(pair(p, value_cols), w.astype(jnp.bfloat16), 0, 0)
            out_t = (mixed / totals).astype(jnp.bfloat16).astype(jnp.float32)
            out = out_t.T.astype(jnp.bfloat16)
            for h in range(groups):
                att_ref[here, head_cols(h)] = out[h * BLOCK : (h + 1) * BLOCK]
            deltas = jnp.sum(out_t * u_t, axis=0, keepdims=True)
            inverse = 1.0 / totals
            query_grad = jnp.zeros((HD, lanes), jnp.float32)
            for p in range(steps):
                prob = s_ref[p] * inverse
                value_part = dot_f32(prob.astype(jnp.bfloat16), u, 1, 0)
                prob_grad = dot_f32(pair(p, value_cols), u, 1, 1)
                ds = (prob * (prob_grad - deltas)).astype(jnp.bfloat16)
                key_part = dot_f32(ds, q, 1, 0) * scale
                query_grad = query_grad + dot_f32(pair(p, key_cols), ds, 0, 0)
                for i in range(2):
                    grads_ref[b, 2 * p + i, :, key_cols] = key_part[i * BLOCK : (i + 1) * BLOCK]
                    grads_ref[b, 2 * p + i, :, value_cols] = value_part[i * BLOCK : (i + 1) * BLOCK]
            qg = (query_grad * scale).T.astype(jnp.bfloat16)
            for h in range(groups):
                qg_ref[here, head_cols(h)] = qg[h * BLOCK : (h + 1) * BLOCK]
        return carry

    lax.fori_loop(0, blocks, one_block, 0)

    release()
    part_ref = kv_ref
    paths = [walk(parents_ref, first + b) for b in range(blocks)]
    block_total = part_ref.shape[0]

    def one_target(target, carry):
        total = jnp.zeros((BLOCK, pair_width), jnp.float32)
        for b in range(blocks):
            depth, path = paths[b]
            slot = jnp.int32(0)
            hits = jnp.int32(0)
            for level in range(DEPTH):
                hit = jnp.where((path[level] == target) & (depth >= level), 1, 0)
                slot = slot + hit * level
                hits = hits + hit
            total = total + grads_ref[b, slot] * hits.astype(jnp.float32)
        part_ref[target] = total.astype(part_ref.dtype)
        return carry

    lax.fori_loop(0, block_total, one_target, 0)


def remote(src, dst, send_sem, recv_sem, ctx, tp):
    return pltpu.make_async_remote_copy(
        src_ref=src,
        dst_ref=dst,
        send_sem=send_sem,
        recv_sem=recv_sem,
        device_id=(ctx, tp),
        device_id_type=MESH,
    )


def greet(devices, count):
    barrier = pltpu.get_barrier_semaphore()
    for ctx, tp, valid in devices:
        if valid is None:
            pl.semaphore_signal(barrier, inc=1, device_id=(ctx, tp), device_id_type=MESH)
        else:

            @pl.when(valid)
            def _():
                pl.semaphore_signal(barrier, inc=1, device_id=(ctx, tp), device_id_type=MESH)

    pl.semaphore_wait(barrier, count)


class PlaneGather:
    def __init__(self, buf, span, chips, relay, sems):
        me, tp = lax.axis_index("ctx"), lax.axis_index("tp")
        self.buf, self.span = buf, span
        self.chips, self.relay = chips, relay and chips == 4
        self.sems = sems
        self.me, self.tp = me, tp
        self.chip, self.core = me // 2, me % 2

    def slot(self, index):
        return self.buf.at[pl.ds(index * self.span, self.span)]

    def holder(self, offset):
        if self.relay:
            along_x = self.chip + (1 - 2 * (self.chip % 2) if offset % 2 else 0)
            return (along_x + (2 if offset >= 2 else 0)) % 4 * 2
        return (self.chip + self.chips - offset) % self.chips * 2

    def out_copy(self, offset):
        peer = (self.chip + offset) % self.chips * 2
        slot = self.slot(self.me)
        if self.relay:
            peer = self.holder(offset)
            if offset == 3:
                one, two = self.holder(1), self.holder(2)
                peer = two * (1 - self.core) + one * self.core
                slot = self.slot(one * (1 - self.core) + two * self.core + self.core)
        return remote(
            slot,
            slot,
            self.sems[0].at[offset],
            self.sems[1].at[offset],
            peer + self.core,
            self.tp,
        )

    def sib_copy(self, offset):
        slot = self.slot(self.holder(offset) + self.core)
        return remote(
            slot,
            slot,
            self.sems[2].at[offset],
            self.sems[3].at[offset],
            self.holder(0) + 1 - self.core,
            self.tp,
        )

    def start(self):
        for offset in range(1, 3 if self.relay else self.chips):
            self.out_copy(offset).start()
        self.sib_copy(0).start()

    def arrive(self, offset):
        self.out_copy(offset).wait_recv()
        if self.relay and offset < 3:

            @pl.when(self.core == offset - 1)
            def _():
                self.out_copy(3).start()

        self.sib_copy(offset).start()
        return self.holder(offset) + self.core

    def arrive_sibling(self, offset):
        self.sib_copy(offset).wait_recv()
        return self.holder(offset) + 1 - self.core

    def drain(self):
        for offset in range(self.chips):
            if offset:
                self.out_copy(offset).wait_send()
            self.sib_copy(offset).wait_send()


class Line:
    def __init__(self, slot_of, size, sems):
        self.ctx, self.tp = lax.axis_index("ctx"), lax.axis_index("tp")
        self.slot_of, self.size, self.sems = slot_of, size, sems

    def send(self, way, k):
        source = self.tp - k if way == 0 else self.tp + k
        valid = (
            (source >= 0) & (self.tp < self.size - 1)
            if way == 0
            else (source < self.size) & (self.tp > 0)
        )
        slot = self.slot_of(source)
        target = self.tp + 1 if way == 0 else self.tp - 1
        return valid, remote(
            slot, slot, self.sems[0].at[way, k], self.sems[1].at[way, k], self.ctx, target
        )

    def start(self, k):
        for way in range(2):
            valid, copy = self.send(way, k)

            @pl.when(valid)
            def _(copy=copy):
                copy.start()

    def arrive(self, k, then):
        for way in range(2):
            source = self.tp - 1 - k if way == 0 else self.tp + 1 + k
            valid = source >= 0 if way == 0 else source < self.size
            slot = self.slot_of(source)

            @pl.when(valid)
            def _(way=way, source=source, slot=slot):
                remote(
                    slot, slot, self.sems[0].at[way, k], self.sems[1].at[way, k], self.ctx, self.tp
                ).wait_recv()
                if k + 1 < self.size - 1:
                    on, copy = self.send(way, k + 1)

                    @pl.when(on)
                    def _():
                        copy.start()

                then(way, source)

    def drain(self):
        for k in range(self.size - 1):
            for way in range(2):
                valid, copy = self.send(way, k)

                @pl.when(valid)
                def _(copy=copy):
                    copy.wait_send()


def sum_grads(
    ctx_size,
    tp_size,
    part_ref,
    cos_ref,
    sin_ref,
    kw_ref,
    vw_ref,
    cols_ref,
    wall,
    weights,
    hg_ref,
    kwg_ref,
    vwg_ref,
    total,
    sib_buf,
    rs_buf,
    gbuf,
    zbuf,
    hg_acc,
    a_sems,
    b_sems,
    g_sems,
    z_sems,
    wait_columns,
):
    me, tp = lax.axis_index("ctx"), lax.axis_index("tp")
    chips = ctx_size // 2
    chip, core = me // 2, me % 2
    rows, pair_width = total.shape
    blocks = sib_buf.shape[1]
    width = hg_ref.shape[1]
    strip = hg_acc.shape[2]
    key_width = pair_width // 2
    sibling = chip * 2 + 1 - core

    def sib_copy(offset):
        target = (chip + offset) % chips
        return remote(
            part_ref.at[pl.ds((target * 2 + 1 - core) * blocks, blocks)],
            sib_buf.at[offset],
            a_sems[0].at[offset],
            a_sems[1].at[offset],
            sibling,
            tp,
        )

    def chip_copy(offset):
        target = (chip + offset) % chips
        return remote(
            sib_buf.at[offset],
            rs_buf.at[offset - 1],
            b_sems[0].at[offset],
            b_sems[1].at[offset],
            target * 2 + core,
            tp,
        )

    order = list(range(1, chips)) + [0]
    for offset in order:
        sib_copy(offset).start()
    for offset in order:
        sib_copy(offset).wait_recv()
        own = part_ref[pl.ds(((chip + offset) % chips * 2 + core) * blocks, blocks)]
        both = own.astype(jnp.float32) + sib_buf[offset].astype(jnp.float32)
        if offset:
            sib_buf[offset] = both.astype(jnp.bfloat16)
            chip_copy(offset).start()
        else:
            total[...] = both.reshape(total.shape)
    for offset in range(1, chips):
        chip_copy(offset).wait_recv()
        total[...] += rs_buf[offset - 1].astype(jnp.float32).reshape(total.shape)
    cosine, sine = cos_ref[...], sin_ref[...]
    for g in range(key_width // HD):
        at = slice(g * HD, (g + 1) * HD)
        x = total[:, at]
        zbuf[tp, :, at] = (x * cosine - pltpu.roll(x, HD // 2, 1) * sine).astype(jnp.bfloat16)
    zbuf[tp, :, key_width:] = total[:, key_width:].astype(jnp.bfloat16)
    gbuf[me] = zbuf[tp]
    line = Line(lambda s: zbuf.at[s], tp_size, z_sems)
    line.start(0)
    grads = PlaneGather(gbuf, 1, chips, True, g_sems)
    grads.start()

    def weight_grad(source, fresh=False):
        left = cols_ref[source]
        key_part = dot_f32(left, gbuf[source, :, :key_width], 1, 0)
        value_part = dot_f32(left, gbuf[source, :, key_width:], 1, 0)
        if fresh:
            kwg_ref[...] = key_part
            vwg_ref[...] = value_part
        else:
            kwg_ref[...] += key_part
            vwg_ref[...] += value_part

    def hidden_grad(source, key_rows, value_rows, fresh=False):
        for n in range(width // strip):
            at = slice(n * strip, (n + 1) * strip)
            part = dot_f32(zbuf[source, :, :key_width], key_rows[at], 1, 1) + dot_f32(
                zbuf[source, :, key_width:], value_rows[at], 1, 1
            )
            part = part.astype(jnp.bfloat16).astype(jnp.float32)
            hg_acc[n] = part if fresh else hg_acc[n] + part

    own = pl.ds(pl.multiple_of(tp * width, 128), width)
    for offset in range(1, ctx_size):
        wait_columns(offset)
    weight_grad(me, True)
    hidden_grad(tp, kw_ref[own, :], vw_ref[own, :], True)
    line.arrive(0, lambda way, source: None)
    for offset in range(1, chips):
        weights.arrive(offset)
    for offset in range(1, chips):
        weight_grad(grads.arrive(offset))
        if offset < tp_size - 1:
            line.arrive(offset, lambda way, source: None)
    for k in range(chips, tp_size - 1):
        line.arrive(k, lambda way, source: None)
    for offset in range(chips):
        weight_grad(grads.arrive_sibling(offset))
    for offset in range(chips):
        weights.arrive_sibling(offset)

    def rows_of(j, matrix):
        pieces = [wall[c, j, matrix] for c in range(ctx_size)]
        if wall.shape[3] % 16:
            pieces = [piece.astype(jnp.float32) for piece in pieces]
        return jnp.concatenate(pieces, axis=0).astype(jnp.bfloat16)

    for j in range(tp_size - 1):
        source = (tp + 1 + j) % tp_size
        hidden_grad(source, rows_of(j, 0), rows_of(j, 1))
    for n in range(width // strip):
        hg_ref[:, n * strip : (n + 1) * strip] = hg_acc[n].astype(jnp.bfloat16)
    for offset in range(chips):
        sib_copy(offset).wait_send()
        if offset:
            chip_copy(offset).wait_send()
    grads.drain()
    weights.drain()
    line.drain()


def layer_kernel(
    ctx_size,
    tp_size,
    parents_ref,
    hid_ref,
    kw_hbm,
    vw_hbm,
    kw_any,
    vw_any,
    q_hbm,
    u_hbm,
    base_ref,
    near_ref,
    att_ref,
    qg_ref,
    hg_ref,
    kwg_ref,
    vwg_ref,
    feat,
    acc,
    kw_ref,
    vw_ref,
    q_ref,
    u_ref,
    kv_ref,
    cols_ref,
    cos_ref,
    sin_ref,
    wall,
    s_ref,
    slot_ref,
    sib_buf,
    rs_buf,
    gbuf,
    zbuf,
    load_sem,
    line_send,
    line_recv,
    col_send,
    col_recv,
    w_send,
    w_recv,
    kv_sems_0,
    kv_sems_1,
    kv_sems_2,
    kv_sems_3,
    wall_sems_0,
    wall_sems_1,
    wall_sems_2,
    wall_sems_3,
    a_sems_0,
    a_sems_1,
    b_sems_0,
    b_sems_1,
    g_sems_0,
    g_sems_1,
    g_sems_2,
    g_sems_3,
    z_send,
    z_recv,
):
    kv_sems = (kv_sems_0, kv_sems_1, kv_sems_2, kv_sems_3)
    wall_sems = (wall_sems_0, wall_sems_1, wall_sems_2, wall_sems_3)
    a_sems = (a_sems_0, a_sems_1)
    b_sems = (b_sems_0, b_sems_1)
    g_sems = (g_sems_0, g_sems_1, g_sems_2, g_sems_3)
    z_sems = (z_send, z_recv)
    me, tp = lax.axis_index("ctx"), lax.axis_index("tp")
    width, rows = hid_ref.shape
    loads = [
        pltpu.make_async_copy(source, held, load_sem.at[i])
        for i, (source, held) in enumerate(
            [(kw_hbm, kw_ref), (vw_hbm, vw_ref), (q_hbm, q_ref), (u_hbm, u_ref)]
        )
    ]
    for load in loads:
        load.start()
    half = width // 2
    key_width = kw_ref.shape[1]
    blocks = rows // BLOCK
    chips = ctx_size // 2
    col_rows = cols_ref.shape[1]
    per_half = half // col_rows
    greet(
        [((me + o) % ctx_size, tp, None) for o in range(1, ctx_size)]
        + [(me, (tp + o) % tp_size, None) for o in range(1, tp_size)],
        ctx_size + tp_size - 2,
    )
    for j in range(2):
        feat[tp, j] = hid_ref[j * half : (j + 1) * half, :]
    lines = [
        Line(lambda s, j=j: feat.at[s, j], tp_size, (line_send.at[j], line_recv.at[j]))
        for j in range(2)
    ]
    lines[0].start(0)

    def col_copy(source, j, i):
        dest = (source * 2 + j) * per_half + i
        offset = (dest + ctx_size - me) % ctx_size
        return dest, remote(
            feat.at[source, j, pl.ds(i * col_rows, col_rows), :],
            cols_ref.at[me],
            col_send.at[offset],
            col_recv.at[offset],
            dest,
            tp,
        )

    def share(source, j):
        for i in range(per_half):
            dest, copy = col_copy(source, j, i)

            @pl.when(dest != me)
            def _(copy=copy):
                copy.start()

            @pl.when(dest == me)
            def _(i=i):
                cols_ref[me] = feat[source, j, i * col_rows : (i + 1) * col_rows, :]

    def project(source, j):
        at = pl.ds(pl.multiple_of(source * width + j * half, 128), half)
        block = feat[source, j]
        acc[:, :key_width] += dot_f32(block, kw_ref[at, :], 0, 0)
        acc[:, key_width:] += dot_f32(block, vw_ref[at, :], 0, 0)

    def wait_columns(offset):
        source = (me + ctx_size - offset) % ctx_size
        slot = cols_ref.at[source]
        remote(slot, slot, col_send.at[offset], col_recv.at[offset], me, tp).wait()

    acc[...] = jnp.zeros_like(acc)
    lines[1].start(0)
    for j in range(2):
        share(tp, j)

    first = me * blocks
    lane = lax.broadcasted_iota(jnp.int32, (BLOCK, HD), 1)
    sign = jnp.where(lane < HD // 2, -1.0, 1.0)
    for b in range(blocks):
        depth, _ = walk(parents_ref, first + b)
        pick = lax.broadcasted_iota(jnp.int32, (DEPTH, HD), 0) == depth
        base_cos = jnp.sum(jnp.where(pick, base_ref[0], 0.0), axis=0, keepdims=True)
        base_sin = jnp.sum(jnp.where(pick, base_ref[1], 0.0), axis=0, keepdims=True)
        at = slice(b * BLOCK, (b + 1) * BLOCK)
        cos_ref[at, :] = base_cos * near_ref[0] - base_sin * near_ref[1]
        sin_ref[at, :] = (base_sin * near_ref[0] + base_cos * near_ref[1]) * sign

    for load in loads[:2]:
        load.wait()
    for j in range(2):
        project(tp, j)
    for j in range(2):
        for k in range(tp_size - 1):
            last = j == 1 and k == tp_size - 2

            def then(way, source, j=j, last=last):
                if not last:
                    share(source, j)
                project(source, j)

            lines[j].arrive(k, then)

    def piece_copy(offset, matrix):
        target = (tp + offset) % tp_size
        return remote(
            (kw_any, vw_any)[matrix].at[target, me],
            wall.at[me, tp_size - 1 - offset, matrix],
            w_send.at[offset, matrix],
            w_recv.at[offset, matrix],
            me,
            target,
        )

    for line in lines:
        line.drain()
    for offset in range(1, tp_size):
        for matrix in range(2):
            piece_copy(offset, matrix).start()

    cosine, sine = cos_ref[...], sin_ref[...]
    for g in range(key_width // HD):
        at = slice(g * HD, (g + 1) * HD)
        x = acc[:, at]
        keys = (x * cosine + pltpu.roll(x, HD // 2, 1) * sine).astype(jnp.bfloat16)
        for b in range(blocks):
            kv_ref[first + b, :, at] = keys[b * BLOCK : (b + 1) * BLOCK]
    for b in range(blocks):
        kv_ref[first + b, :, key_width:] = acc[
            b * BLOCK : (b + 1) * BLOCK, key_width:
        ].astype(jnp.bfloat16)
    gather = PlaneGather(kv_ref, blocks, chips, True, kv_sems)
    gather.start()
    for offset in range(1, chips):
        gather.arrive(offset)
    k = tp_size - 2
    for way in range(2):
        source = tp - 1 - k if way == 0 else tp + 1 + k
        valid = source >= 0 if way == 0 else source < tp_size

        @pl.when(valid)
        def _(source=source):
            share(source, 1)

    for offset in range(chips):
        gather.arrive_sibling(offset)
    for offset in range(1, tp_size):
        for matrix in range(2):
            piece_copy(offset, matrix).wait()
    weights = PlaneGather(wall, 1, chips, False, wall_sems)
    weights.start()
    for load in loads[2:]:
        load.wait()
    attend(parents_ref, kv_ref, q_ref, u_ref, att_ref, qg_ref, s_ref, slot_ref, gather.drain)
    sum_grads(
        ctx_size,
        tp_size,
        kv_ref,
        cos_ref,
        sin_ref,
        kw_ref,
        vw_ref,
        cols_ref,
        wall,
        weights,
        hg_ref,
        kwg_ref,
        vwg_ref,
        acc,
        sib_buf,
        rs_buf,
        gbuf,
        zbuf,
        s_ref,
        a_sems,
        b_sems,
        g_sems,
        z_sems,
        wait_columns,
    )


def rope_tables():
    lane = jnp.arange(HD, dtype=jnp.int32) % (HD // 2)
    frequency = jnp.exp(lane.astype(jnp.float32) * (-2.0 * math.log(THETA) / HD))
    base = (jnp.arange(DEPTH, dtype=jnp.int32) * BLOCK).astype(jnp.float32)[:, None] * frequency
    near = jnp.arange(BLOCK, dtype=jnp.int32).astype(jnp.float32)[:, None] * frequency
    return (
        jnp.stack([jnp.cos(base), jnp.sin(base)]),
        jnp.stack([jnp.cos(near), jnp.sin(near)]),
    )


def shards(ctx_size, tp_size, hidden, queries, key_weight, value_weight, parents, upstream):
    rows, width = hidden.shape
    depth_rows, key_width = key_weight.shape
    pair_width = 2 * key_width
    col_rows = depth_rows // ctx_size
    piece_rows = width // ctx_size
    chips = ctx_size // 2
    vmem = pl.BlockSpec(memory_space=pltpu.VMEM)
    anywhere = pl.BlockSpec(memory_space=pl.ANY)
    smem = pl.BlockSpec(memory_space=pltpu.SMEM)
    bf16, f32 = jnp.bfloat16, jnp.float32
    dma = pltpu.SemaphoreType.DMA
    base, near = rope_tables()
    split = (tp_size, ctx_size, piece_rows, key_width)

    out_types = (
        jax.ShapeDtypeStruct(queries.shape, bf16),
        jax.ShapeDtypeStruct(queries.shape, bf16),
        jax.ShapeDtypeStruct(hidden.shape, bf16),
        jax.ShapeDtypeStruct((col_rows, key_width), f32),
        jax.ShapeDtypeStruct((col_rows, key_width), f32),
    )
    return pl.pallas_call(
        partial(layer_kernel, ctx_size, tp_size),
        name="layer",
        out_shape=out_types,
        in_specs=[smem, vmem] + [anywhere] * 6 + [vmem] * 2,
        out_specs=(vmem,) * 5,
        scratch_shapes=[
            pltpu.VMEM((tp_size, 2, width // 2, rows), bf16),
            pltpu.VMEM((rows, pair_width), f32),
            pltpu.VMEM(key_weight.shape, bf16),
            pltpu.VMEM(key_weight.shape, bf16),
            pltpu.VMEM(queries.shape, bf16),
            pltpu.VMEM(queries.shape, bf16),
            pltpu.VMEM((ctx_size * rows // BLOCK, BLOCK, pair_width), bf16),
            pltpu.VMEM((ctx_size, col_rows, rows), bf16),
            pltpu.VMEM((rows, HD), f32),
            pltpu.VMEM((rows, HD), f32),
            pltpu.VMEM((ctx_size, tp_size - 1, 2, piece_rows, key_width), bf16),
            pltpu.VMEM((DEPTH // 2, 2 * BLOCK, width // key_width * BLOCK), f32),
            pltpu.VMEM((rows // BLOCK, DEPTH, BLOCK, pair_width), f32),
            pltpu.VMEM((chips, rows // BLOCK, BLOCK, pair_width), bf16),
            pltpu.VMEM((chips - 1, rows // BLOCK, BLOCK, pair_width), bf16),
            pltpu.VMEM((ctx_size, rows, pair_width), bf16),
            pltpu.VMEM((tp_size, rows, pair_width), bf16),
            dma((4,)),
            dma((2, 2, tp_size - 1)),
            dma((2, 2, tp_size - 1)),
            dma((ctx_size,)),
            dma((ctx_size,)),
            dma((tp_size, 2)),
            dma((tp_size, 2)),
        ]
        + [dma((chips,))] * 16
        + [dma((2, tp_size - 1))] * 2,
        compiler_params=pltpu.CompilerParams(
            collective_id=1, has_side_effects=True, vmem_limit_bytes=VMEM_LIMIT
        ),
    )(
        parents,
        hidden.T,
        key_weight,
        value_weight,
        key_weight.reshape(split),
        value_weight.reshape(split),
        queries,
        upstream,
        base,
        near,
    )


def solution(mesh):
    return jax.shard_map(
        partial(shards, mesh.shape["ctx"], mesh.shape["tp"]),
        mesh=mesh,
        in_specs=(
            P("ctx", "tp"),
            P("ctx", "tp"),
            P(None, "tp"),
            P(None, "tp"),
            P(),
            P("ctx", "tp"),
        ),
        out_specs=(P("ctx", "tp"),) * 5,
        check_vma=False,
    )
```

time: 173 us -> 159 us (0.919)
  the two profiles are of different devices: /device:TPU:0 before, /device:TPU:7 now
where the time goes in v3:
time: 159 us
  Pallas kernels  148 us (93%)
  local copies, waits for them, and re-layouts  8.75 us (6%)
  other arithmetic  1.7 us (1%)
    pallas_call x1, Pallas kernels, shards(): pl.pallas_call(partial(layer_kernel, ctx_size, tp_size), name='layer', ou...  148 us
    unnamed x12, local copies, waits for them, and re-layouts  8.75 us

profile of v3, /device:TPU:7, one launch (start us, length us, event | category | flops | bytes accessed | tf_op | source)
XLA Modules:
  0.0 158.9 jit_solution(3199538105684389156)
XLA Ops:
  0.7 0.1 multiply_cosine_fusion.1
  0.8 0.6 pad_maximum_fusion.1.base_ref
  1.4 0.3 multiply_cosine_fusion
  1.7 0.7 pad_maximum_fusion.near_ref
  2.4 2.2 %copy.11 = bf16[256,1280]{0,1:T(8,128)(2,1)} copy(bf16[256,1280]{1,0:T(8,128)(2,1)} %param.6) | data formatting | bytes 1310720 | tf_op args[0]
  4.5 147.8 %layer.1 = (bf16[256,1280]{1,0:T(8,128)(2,1)}, bf16[256,1280]{1,0:T(8,128)(2,1)}, bf16[256,1280]{1,0:T(8,128)(2,1)}, f32[640,256]{1,0:T(8,128)}, f32[640,256]{1,0:T(8,128)}) custom-call(s32[16]{0:T(128)} %parents_ref.1, bf16[1280,256]{1,0:T(8,128)(2,1)} %bitcast.5, bf16[5120,256]{1,0:T(8,128)(2,1)} %kw_hbm.1, bf16[5120,256]{1,0:T(8,128)(2,1)} %vw_hbm.1, ...), custom_call_target="tpu_custom_call" | custom-call | tf_op jit(solution)/shard_map/layer/pallas_call | solution.py:715
  152.3 0.0 copy-start.2
  152.3 0.0 copy-start.1
  152.3 0.0 copy-start
  152.4 2.1 %copy.17 = bf16[256,1280]{1,0:T(8,128)(2,1)} copy(bf16[256,1280]{1,0:T(8,128)(2,1)} %get-tuple-element.14) | data formatting | bytes 1310720
  154.5 2.0 %copy.18 = bf16[256,1280]{1,0:T(8,128)(2,1)} copy(bf16[256,1280]{1,0:T(8,128)(2,1)} %get-tuple-element.15) | data formatting | bytes 1310720
  156.4 0.0 copy-done.2
  156.4 0.8 copy.19
  157.3 0.0 copy-done.1
  157.3 0.8 copy.20
  158.1 0.0 copy-done
  158.1 0.8 copy.21
  (3 shorter events, 0.0 us)
Async XLA Ops:
  152.3 4.1 %copy-start.2 = (bf16[256,1280]{1,0:T(8,128)(2,1)S(1)}, bf16[256,1280]{1,0:T(8,128)(2,1)}, u32[]{:S(2)}) copy-start(bf16[256,1280]{1,0:T(8,128)(2,1)} %get-tuple-element.16) | copy-start | bytes 1966084
  152.3 4.9 %copy-start.1 = (f32[640,256]{1,0:T(8,128)S(1)}, f32[640,256]{1,0:T(8,128)}, u32[]{:S(2)}) copy-start(f32[640,256]{1,0:T(8,128)} %get-tuple-element.17) | copy-start | bytes 1966084
  152.3 5.8 %copy-start = (f32[640,256]{1,0:T(8,128)S(1)}, f32[640,256]{1,0:T(8,128)}, u32[]{:S(2)}) copy-start(f32[640,256]{1,0:T(8,128)} %get-tuple-element.18) | copy-start | bytes 1966084

commit v4 on v3

--- a/solution.py
+++ b/solution.py
@@ -318,6 +318,7 @@
     g_sems,
     z_sems,
     wait_columns,
+    start_weights,
 ):
     me, tp = lax.axis_index("ctx"), lax.axis_index("tp")
     chips = ctx_size // 2
@@ -377,6 +378,7 @@
     line.start(0)
     grads = PlaneGather(gbuf, 1, chips, True, g_sems)
     grads.start()
+    start_weights()
 
     def weight_grad(source, fresh=False):
         left = cols_ref[source]
@@ -405,11 +407,10 @@
     hidden_grad(tp, kw_ref[own, :], vw_ref[own, :], True)
     line.arrive(0, lambda way, source: None)
     for offset in range(1, chips):
-        weights.arrive(offset)
-    for offset in range(1, chips):
         weight_grad(grads.arrive(offset))
         if offset < tp_size - 1:
             line.arrive(offset, lambda way, source: None)
+        weights.arrive(offset)
     for k in range(chips, tp_size - 1):
         line.arrive(k, lambda way, source: None)
     for offset in range(chips):
@@ -643,11 +644,14 @@
 
     for offset in range(chips):
         gather.arrive_sibling(offset)
-    for offset in range(1, tp_size):
-        for matrix in range(2):
-            piece_copy(offset, matrix).wait()
-    weights = PlaneGather(wall, 1, chips, False, wall_sems)
-    weights.start()
+    weights = PlaneGather(wall, 1, chips, True, wall_sems)
+
+    def start_weights():
+        for offset in range(1, tp_size):
+            for matrix in range(2):
+                piece_copy(offset, matrix).wait()
+        weights.start()
+
     for load in loads[2:]:
         load.wait()
     attend(parents_ref, kv_ref, q_ref, u_ref, att_ref, qg_ref, s_ref, slot_ref, gather.drain)
@@ -676,6 +680,7 @@
         g_sems,
         z_sems,
         wait_columns,
+        start_weights,
     )
 
 

time: 159 us -> 147 us (0.925)
  the two profiles are of different devices: /device:TPU:7 before, /device:TPU:0 now
where the time goes in v4:
time: 147 us; the launch traced here: 146 us
  Pallas kernels  135 us (92%)
  local copies, waits for them, and re-layouts  8.75 us (6%)
  other arithmetic  1.7 us (1%)
    pallas_call x1, Pallas kernels, shards(): pl.pallas_call(partial(layer_kernel, ctx_size, tp_size), name='layer', ou...  135 us
    unnamed x12, local copies, waits for them, and re-layouts  8.75 us

profile of v4, /device:TPU:0, one launch (start us, length us, event | category | flops | bytes accessed | tf_op | source)
XLA Modules:
  0.0 145.8 jit_solution(11655878554283137180)
XLA Ops:
  0.7 0.1 multiply_cosine_fusion.1
  0.8 0.6 pad_maximum_fusion.1.base_ref
  1.4 0.3 multiply_cosine_fusion
  1.7 0.7 pad_maximum_fusion.near_ref
  2.4 2.2 %copy.11 = bf16[256,1280]{0,1:T(8,128)(2,1)} copy(bf16[256,1280]{1,0:T(8,128)(2,1)} %param.6) | data formatting | bytes 1310720 | tf_op args[0]
  4.5 134.6 %layer.1 = (bf16[256,1280]{1,0:T(8,128)(2,1)}, bf16[256,1280]{1,0:T(8,128)(2,1)}, bf16[256,1280]{1,0:T(8,128)(2,1)}, f32[640,256]{1,0:T(8,128)}, f32[640,256]{1,0:T(8,128)}) custom-call(s32[16]{0:T(128)} %parents_ref.1, bf16[1280,256]{1,0:T(8,128)(2,1)} %bitcast.5, bf16[5120,256]{1,0:T(8,128)(2,1)} %kw_hbm.1, bf16[5120,256]{1,0:T(8,128)(2,1)} %vw_hbm.1, ...), custom_call_target="tpu_custom_call" | custom-call | tf_op jit(solution)/shard_map/layer/pallas_call | solution.py:720
  139.1 0.0 copy-start.2
  139.2 0.0 copy-start.1
  139.2 0.0 copy-start
  139.2 2.1 %copy.17 = bf16[256,1280]{1,0:T(8,128)(2,1)} copy(bf16[256,1280]{1,0:T(8,128)(2,1)} %get-tuple-element.14) | data formatting | bytes 1310720
  141.3 2.0 %copy.18 = bf16[256,1280]{1,0:T(8,128)(2,1)} copy(bf16[256,1280]{1,0:T(8,128)(2,1)} %get-tuple-element.15) | data formatting | bytes 1310720
  143.2 0.0 copy-done.2
  143.2 0.8 copy.19
  144.1 0.0 copy-done.1
  144.1 0.8 copy.20
  144.9 0.0 copy-done
  144.9 0.8 copy.21
  (3 shorter events, 0.0 us)
Async XLA Ops:
  139.1 4.1 %copy-start.2 = (bf16[256,1280]{1,0:T(8,128)(2,1)S(1)}, bf16[256,1280]{1,0:T(8,128)(2,1)}, u32[]{:S(2)}) copy-start(bf16[256,1280]{1,0:T(8,128)(2,1)} %get-tuple-element.16) | copy-start | bytes 1966084
  139.2 4.9 %copy-start.1 = (f32[640,256]{1,0:T(8,128)S(1)}, f32[640,256]{1,0:T(8,128)}, u32[]{:S(2)}) copy-start(f32[640,256]{1,0:T(8,128)} %get-tuple-element.17) | copy-start | bytes 1966084
  139.2 5.8 %copy-start = (f32[640,256]{1,0:T(8,128)S(1)}, f32[640,256]{1,0:T(8,128)}, u32[]{:S(2)}) copy-start(f32[640,256]{1,0:T(8,128)} %get-tuple-element.18) | copy-start | bytes 1966084
